TPU v7x, 512 devices: a whole 4x4x16 slice. The times are simulated.
512 devices in a mesh: seq: 64 (over y, z), head: 8 (over x, core).
Axes of the slice: x: 4, y: 4, z: 16, core: 2. Of those that a mesh axis runs over, the one named last changes fastest.
Arguments:
- head_input: bfloat16 [16384, 8192], P('seq', 'head'), may hold values from -6 to 6
- out_grad: bfloat16 [16384, 8192], P('seq', 'head'), may hold values from -6 to 6
- b_proj: bfloat16 [16384, 1024], P('seq', 'head'), may hold values from -6 to 6
- c_proj: bfloat16 [16384, 1024], P('seq', 'head'), may hold values from -6 to 6
- time_step: float32 [128, 16384], P('head', 'seq'), may hold values from 0.0005 to 0.0015
- decay_log: float32 [128], P('head'), may hold values from -7 to 4, as said below
- skip_gain: float32 [128], P('head'), may hold values from 0.5 to 1.5
- layer_input: bfloat16 [16384, 4096], P('seq', 'head'), may hold values from -6 to 6
Outputs:
- input_grad: bfloat16 [16384, 8192], P('seq', 'head')
- bc_grad: float32 [16384, 2048], P('seq', 'head')
- weight_grad: float32 [8, 256, 4096], P('head', 'seq')
Inputs may be any that keep to these rules, and one draw needn't show every extreme that they name: decay_log is the logarithm of a positive rate of each head.
All inputs are finite; a program needn't handle non-finite values.
Results may differ from a plain program's by a relative error of at most 0.0064.
Values may be sent and summed in bfloat16 or wider, within the bound.
No kernel may reach another device: no remote copies, remote signals or barrier semaphores. Data moves between devices by JAX's collectives and lax.ppermute only.
A program may use at most 192 MiB of HBM per device.

v0:
```python
import jax
import jax.numpy as jnp
from jax import lax
from jax.sharding import PartitionSpec as P

BLOCK = 256


def carried_in(x, axis, combine, identity, reverse):
    size, here = (lax.axis_size(axis), lax.axis_index(axis))
    everything = jax.tree.map(lambda part: lax.all_gather(part, axis), x)
    start = jax.tree.map(
        lambda part, zero: jnp.broadcast_to(jnp.asarray(zero, part.dtype), part.shape), x, identity
    )

    def hop(k, before):
        at = size - 1 - k if reverse else k
        reached = at > here if reverse else at < here
        new = combine(before, jax.tree.map(lambda part: part[at], everything))
        return jax.tree.map(lambda a, b: jnp.where(reached, a, b), new, before)

    return lax.fori_loop(0, size, hop, start)


def outer_rows(left, right):
    return lax.dot_general(
        left, right, (((0,), (0,)), ((), ())), preferred_element_type=jnp.float32
    )


def expand_heads(final_log, head_dim):
    return jnp.repeat(jnp.exp(final_log), head_dim)[:, None]


def block_terms(head_block, grad_block, step_block, decay_rates, head_dim):
    log_decay = step_block * decay_rates[:, None]
    cumulative = jnp.cumsum(log_decay, axis=1)
    final_log = cumulative[:, -1]
    input_weight = jnp.exp(final_log[:, None] - cumulative) * step_block
    column_weight = jnp.repeat(input_weight.T, head_dim, axis=1)
    grad_weight = jnp.repeat(jnp.exp(cumulative).T, head_dim, axis=1)
    scaled_input = (head_block * column_weight).astype(jnp.bfloat16)
    scaled_grad = (grad_block * grad_weight).astype(jnp.bfloat16)
    return (cumulative, final_log, column_weight, scaled_input, scaled_grad)


def block_grads(
    head_block,
    grad_block,
    b_block,
    c_block,
    step_block,
    terms,
    start_state,
    end_state,
    skip_columns,
    head_dim,
):
    cumulative, final_log, column_weight, scaled_input, scaled_grad = terms
    block_len = head_block.shape[0]
    group_heads = step_block.shape[0]
    heads_three = head_block.reshape(block_len, group_heads, head_dim)
    grads_three = grad_block.reshape(block_len, group_heads, head_dim)
    scores = jnp.dot(c_block, b_block.T, preferred_element_type=jnp.float32)
    positions = jnp.arange(block_len)
    causal = positions[:, None] >= positions[None, :]
    gaps = cumulative[:, :, None] - cumulative[:, None, :]
    decay_matrix = (
        jnp.where(causal, jnp.exp(jnp.where(causal, gaps, 0.0)), 0.0) * step_block[:, None, :]
    )
    transfer = (scores[None] * decay_matrix).astype(jnp.bfloat16)
    inner_grad = jnp.einsum(
        "hsr,shp->rhp", transfer, grads_three, preferred_element_type=jnp.float32
    ).reshape(block_len, -1)
    pairs = jnp.einsum("shp,rhp->hsr", grads_three, heads_three, preferred_element_type=jnp.float32)
    mixed = jnp.sum(pairs * decay_matrix, axis=0).astype(jnp.bfloat16)
    start_low = start_state.astype(jnp.bfloat16)
    end_low = end_state.astype(jnp.bfloat16)
    carried = jnp.dot(b_block, end_low.T, preferred_element_type=jnp.float32) * column_weight
    input_grad = (skip_columns * grad_block + inner_grad + carried).astype(jnp.bfloat16)
    grad_b = jnp.dot(mixed.T, c_block, preferred_element_type=jnp.float32)
    grad_b = grad_b + jnp.dot(scaled_input, end_low, preferred_element_type=jnp.float32)
    grad_c = jnp.dot(mixed, b_block, preferred_element_type=jnp.float32)
    grad_c = grad_c + jnp.dot(scaled_grad, start_low, preferred_element_type=jnp.float32)
    return (input_grad, jnp.concatenate([grad_b, grad_c], axis=1))


def local(head_input, out_grad, b_proj, c_proj, time_step, decay_log, skip_gain, layer_input):
    tokens = head_input.shape[0]
    group_heads = time_step.shape[0]
    head_dim = head_input.shape[1] // group_heads
    state_size = b_proj.shape[1]
    blocks = tokens // BLOCK
    decay_rates = -jnp.exp(decay_log)
    skip_columns = jnp.repeat(skip_gain, head_dim)[None, :]
    block_index = 0
    terms = block_terms(head_input, out_grad, time_step, decay_rates, head_dim)
    state_in = outer_rows(terms[3], b_proj)
    state_grad = outer_rows(terms[4], c_proj)
    pieces = [(head_input, out_grad, b_proj, c_proj, time_step, terms, state_in, state_grad)]
    empty_state = jnp.zeros((group_heads * head_dim, state_size), jnp.float32)
    local_state = empty_state
    local_grad = empty_state
    item = pieces[0]
    local_state = expand_heads(item[5][1], head_dim) * local_state + item[6]
    local_log = item[5][1]
    for item in reversed(pieces):
        local_grad = item[7] + expand_heads(item[5][1], head_dim) * local_grad

    def combine_states(earlier, later):
        return (earlier[0] + later[0], expand_heads(later[0], head_dim) * earlier[1] + later[1])

    identity = (jnp.zeros((group_heads,), jnp.float32), empty_state)
    start_device = carried_in((local_log, local_state), "seq", combine_states, identity, False)[1]
    end_device = carried_in((local_log, local_grad), "seq", combine_states, identity, True)[1]
    current = start_device
    block_starts = [current]
    block_ends = [empty_state] * blocks
    current = end_device
    for block_index in reversed(range(blocks)):
        block_ends[block_index] = current
        current = (
            pieces[block_index][7] + expand_heads(pieces[block_index][5][1], head_dim) * current
        )
    block_index = 0
    item = pieces[block_index]
    input_part, bc_part = block_grads(
        item[0],
        item[1],
        item[2],
        item[3],
        item[4],
        item[5],
        block_starts[block_index],
        block_ends[block_index],
        skip_columns,
        head_dim,
    )
    bc_low = bc_part.astype(jnp.bfloat16)
    total_length = tokens * lax.axis_size("seq")
    weight_term = (
        outer_rows(bc_low, lax.all_gather(layer_input, "head", axis=1, tiled=True)) / total_length
    )
    weight_part = lax.psum_scatter(weight_term, "seq", scatter_dimension=0, tiled=True)
    return (input_part, bc_part, weight_part[None])


def solution(mesh):
    in_specs = (
        P("seq", "head"),
        P("seq", "head"),
        P("seq", "head"),
        P("seq", "head"),
        P("head", "seq"),
        P("head"),
        P("head"),
        P("seq", "head"),
    )
    out_specs = (P("seq", "head"), P("seq", "head"), P("head", "seq", None))
    return jax.shard_map(local, mesh=mesh, in_specs=in_specs, out_specs=out_specs, check_vma=False)
```

profile of v0, /device:TPU:2, one launch (start us, length us, event | category | flops | bytes accessed | tf_op | source)
XLA Modules:
  0.0 1004.2 jit_solution(14977482159689368856)
XLA Ops:
  12.1 1.9 convolution_add_fusion.1
  16.5 1.7 multiply_reduce_fusion
  20.3 151.3 %all-reduce = f32[1024]{0:T(1024)S(1)} all-reduce(f32[1024]{0:T(1024)S(1)} %dynamic-update-slice), channel_id=2, replica_groups=mesh['seq'=64,'head'=8] {'seq'}, use_global_device_ids=true, to_apply=%add | all-reduce | flops 1024 | bytes 8192
  171.6 141.3 %all-gather.9.cloned.1.call-done = f32[65536,128]{1,0:T(8,128)} async-done(((f32[1024,128]{1,0:T(8,128)}), f32[65536,128]{1,0:T(8,128)}) %all-gather.9.cloned.1.call-update) | async-done | bytes 33554448 | tf_op jit(solution)/shard_map/all_gather | solution.py:11
  312.9 98.7 %while.30 = (s32[]{:T(128)}, f32[1024,128]{1,0:T(8,128)S(1)}, s32[]{:T(128)}, f32[64,16]{1,0:T(8,128)S(1)}, f32[64,1024,128]{2,1,0:T(8,128)}, /*index=5*/s32[]{:T(128)}, s32[]{:T(128)}, s32[]{:T(128)}, s32[]{:T(128)}) while((s32[]{:T(128)}, f32[1024,128]{1,0:T(8,128)S(1)}, s32[]{:T(128)}, f32[64,16]{1,0:T(8,128)S(1)}, ...), condition=%wide.region_3.4_spmd.clone, body=%wide.region_2.3_spmd.clone.sunk | while | flops 524296 | bytes 1589607 | solution.py:22
  313.0 1.3 fusion.46
  314.6 1.3 fusion.46
  316.1 1.3 fusion.46
  320.7 1.3 fusion.46
  322.3 1.3 fusion.46
  323.8 1.3 fusion.46
  326.9 1.4 fusion.46
  328.4 1.4 fusion.46
  333.0 1.3 fusion.46
  334.6 1.3 fusion.46
  336.1 1.3 fusion.46
  337.6 1.3 fusion.46
  339.2 1.3 fusion.46
  342.3 1.4 fusion.46
  345.3 1.3 fusion.46
  346.9 1.3 fusion.46
  349.9 1.3 fusion.46
  351.5 1.3 fusion.46
  353.0 1.3 fusion.46
  354.6 1.3 fusion.46
  359.2 1.4 fusion.46
  360.7 1.4 fusion.46
  362.3 1.3 fusion.46
  365.3 1.3 fusion.46
  366.9 1.4 fusion.46
  370.0 1.3 fusion.46
  371.5 1.4 fusion.46
  376.1 1.3 fusion.46
  377.7 1.4 fusion.46
  379.2 1.4 fusion.46
  380.7 1.4 fusion.46
  382.3 1.4 fusion.46
  385.4 1.3 fusion.46
  386.9 1.3 fusion.46
  388.4 1.3 fusion.46
  390.0 1.3 fusion.46
  391.5 1.3 fusion.46
  396.1 1.3 fusion.46
  397.7 1.3 fusion.46
  403.8 1.3 fusion.46
  405.3 1.5 fusion.46
  407.0 1.4 fusion.46
  408.6 1.4 fusion.46
  410.2 1.4 fusion.46
  411.6 194.9 %all-gather.11.cloned.1.call-done = f32[65536,128]{1,0:T(8,128)} async-done(((f32[1024,128]{1,0:T(8,128)}), f32[65536,128]{1,0:T(8,128)}) %all-gather.11.cloned.1.call-update) | async-done | bytes 33554448 | tf_op jit(solution)/shard_map/all_gather | solution.py:11
  606.5 97.9 %while.31 = (s32[]{:T(128)}, f32[1024,128]{1,0:T(8,128)S(1)}, s32[]{:T(128)}, f32[64,16]{1,0:T(8,128)S(1)}, f32[64,1024,128]{2,1,0:T(8,128)}, /*index=5*/s32[]{:T(128)}, s32[]{:T(128)}) while((s32[]{:T(128)}, f32[1024,128]{1,0:T(8,128)S(1)}, s32[]{:T(128)}, f32[64,16]{1,0:T(8,128)S(1)}, f32[64,1024,128]{2,1,0:T(8,128)}, ...), condition=%wide.region_6.7_spmd.clone, body=%wide.region_5.6_spmd.clone.sunk | while | flops 524292 | bytes 1589545 | solution.py:22
  606.7 1.3 fusion.47
  620.4 1.4 fusion.47
  622.0 1.4 fusion.47
  626.6 1.4 fusion.47
  628.1 1.3 fusion.47
  631.2 1.4 fusion.47
  632.7 1.4 fusion.47
  635.8 1.4 fusion.47
  705.0 4.2 convolution_multiply_fusion
  710.3 2.5 fusion.2
  713.7 1.6 fusion.10
  716.2 279.9 %all-reduce.4.cloned.1.call-done = f32[256,4096]{1,0:T(8,128)} async-done(((f32[256,4096]{1,0:T(8,128)}), f32[256,4096]{1,0:T(8,128)}) %all-reduce.4.cloned.1.call-update) | async-done | bytes 4194320
  996.1 1.5 dynamic-slice_bitcast_fusion
  (515 shorter events, 133.4 us)
Async XLA Ops:
  7.2 7.3 copy-start
  7.2 9.3 copy-start.3
  7.2 6.9 copy-start.2
  7.2 305.7 %all-gather.9.cloned.1.call-start = ((), (), s32[]{:S(2)}) async-start(), calls=%async_computation.1 | async-start | bytes 34078720 | tf_op jit(solution)/shard_map/all_gather | solution.py:11
  14.1 592.4 %all-gather.11.cloned.1.call-start = ((), (), s32[]{:S(2)}) async-start(), calls=%async_computation.2 | async-start | bytes 34078720 | tf_op jit(solution)/shard_map/all_gather | solution.py:11
  15.6 689.4 %all-gather.7.cloned.1.call-start = ((), (), s32[]{:S(2)}) async-start(), calls=%async_computation | async-start | bytes 2359296 | tf_op jit(solution)/shard_map/all_gather | solution.py:142
  16.3 979.8 %all-reduce.4.cloned.1.call-start = ((), (), s32[]{:S(2)}) async-start(), calls=%async_computation.3 | async-start | bytes 8388608
  16.5 1.8 copy-start.1
  16.5 2.2 copy-start.4
  705.0 4.3 copy-start.5
Sparse Core Ops, SparseCore 0:
  14.2 298.6 all-gather.8
  315.8 290.6 all-gather.10
  608.6 28.3 all-gather.6
  709.4 286.6 all-reduce.3
where the time goes:
time: 1010 us; the launch traced here: 1000 us
  waiting for transfers between devices  617 us (61%)
  other arithmetic  176 us (17%)
  blocking collectives  151 us (15%)
  local copies, waits for them, and re-layouts  26.3 us (3%)
  between operations  15.4 us (2%)
  matrix products  14.2 us (1%)
    all_gather x2, waiting for transfers between devices, carried_in(): everything = jax.tree.map(lambda part: lax.all_gather(part, axis), x)  336 us
    unnamed x5, waiting for transfers between devices  281 us
    select_n x128, other arithmetic, hop(): return jax.tree.map(lambda a, b: jnp.where(reached, a, b), new, before)  173 us
    unnamed x1, blocking collectives  151 us
  transfers between devices with their start and end apart: 4, of which 3 were waited for; matrix products, arithmetic and copies ran while one was open for 20% of the time, Pallas kernels for 0%

commit v1 on v0

v1 whole, which is shorter than its diff:
```python
import jax
import jax.numpy as jnp
from jax import lax
from jax.sharding import Mesh, PartitionSpec as P

Y, Z, X, CORE = 4, 16, 4, 2
BLOCK = 256
HEADS = 16
DIM = 64
STATE = 128
bf16 = jnp.bfloat16
f32 = jnp.float32


def rows_dot(left, right):
    return lax.dot_general(left, right, (((0,), (0,)), ((), ())), preferred_element_type=f32)


def to_chunks(state):
    return state.reshape(2, 64, 8, 128).transpose(2, 0, 1, 3).reshape(16, 64, 128)


def from_chunks(chunks):
    return chunks.reshape(8, 2, 64, 128).transpose(1, 2, 0, 3).reshape(128, 1024)


def pieces_of(value):
    high = value.astype(bf16)
    rest = value - high.astype(f32)
    mid = rest.astype(bf16)
    low = (rest - mid.astype(f32)).astype(bf16)
    return high, mid, low


def local(head_input, out_grad, b_proj, c_proj, time_step, decay_log, skip_gain, layer_input):
    everything = lax.all_gather(layer_input, ("y", "x", "core"))
    rates = -jnp.exp(decay_log)
    cum = jnp.cumsum(time_step * rates[:, None], axis=1)
    last = cum[:, -1]
    coef = jnp.exp(last[:, None] - cum) * time_step
    col_weight = jnp.repeat(coef.T, DIM, axis=1)
    grad_weight = jnp.repeat(jnp.exp(cum).T, DIM, axis=1)
    xs = (head_input * col_weight).astype(bf16)
    dys = (out_grad * grad_weight).astype(bf16)
    state_in = to_chunks(rows_dot(b_proj, xs))
    state_grad = to_chunks(rows_dot(c_proj, dys))
    lane_log = jnp.repeat(jnp.repeat(last, DIM).reshape(8, 1, 128), 2, axis=0)
    high, mid, low = pieces_of(lane_log)
    packed = jnp.concatenate(
        [state_in.astype(bf16), state_grad.astype(bf16), high, mid, low, jnp.zeros((16, 5, 128), bf16)], axis=1
    )
    got = lax.all_to_all(packed, "z", 0, 0, tiled=True)

    heads_three = head_input.reshape(BLOCK, HEADS, DIM)
    grads_three = out_grad.reshape(BLOCK, HEADS, DIM)
    scores = jnp.dot(c_proj, b_proj.T, preferred_element_type=f32)
    positions = jnp.arange(BLOCK)
    causal = positions[:, None] >= positions[None, :]
    gaps = cum[:, :, None] - cum[:, None, :]
    decay = jnp.where(causal, jnp.exp(jnp.where(causal, gaps, 0.0)), 0.0) * time_step[:, None, :]
    transfer = (scores[None] * decay).astype(bf16)
    inner = jnp.einsum("hsr,shp->rhp", transfer, grads_three, preferred_element_type=f32).reshape(BLOCK, -1)
    pairs = jnp.einsum("shp,rhp->hsr", grads_three, heads_three, preferred_element_type=f32)
    mixed = jnp.sum(pairs * decay, axis=0).astype(bf16)
    grad_b = jnp.dot(mixed.T, c_proj, preferred_element_type=f32)
    grad_c = jnp.dot(mixed, b_proj, preferred_element_type=f32)
    inner = inner + jnp.repeat(skip_gain, DIM)[None, :] * out_grad

    logs = jnp.sum(got[:, 128:131].astype(f32), axis=1, keepdims=True)
    fwd = got[:, :64].astype(f32)
    bwd = got[:, 64:128].astype(f32)
    decays = jnp.exp(logs)
    starts = [jnp.zeros((64, 128), f32)]
    for z in range(Z):
        starts.append(decays[z] * starts[-1] + fwd[z])
    ends = [jnp.zeros((64, 128), f32)]
    for z in reversed(range(Z)):
        ends.append(decays[z] * ends[-1] + bwd[z])
    row_log = jnp.sum(logs, axis=0)
    totals = jnp.concatenate([starts[-1], ends[-1], row_log, jnp.zeros((7, 128), f32)], axis=0)
    rows = lax.all_gather(totals, "y")
    here = lax.axis_index("y")
    row_decays = jnp.exp(rows[:, 128:129])
    carry = jnp.zeros((64, 128), f32)
    carry_end = jnp.zeros((64, 128), f32)
    for y in range(Y - 1):
        carry = jnp.where(y < here, row_decays[y] * carry + rows[y, :64], carry)
        up = Y - 1 - y
        carry_end = jnp.where(up > here, row_decays[up] * carry_end + rows[up, 64:128], carry_end)
    before = jnp.exp(jnp.cumsum(logs, axis=0) - logs)
    after = jnp.exp(row_log[None] - jnp.cumsum(logs, axis=0))
    start_all = jnp.stack(starts[:Z]) + before * carry[None]
    end_all = jnp.stack(ends[:Z][::-1]) + after * carry_end[None]
    back = jnp.concatenate([start_all.astype(bf16), end_all.astype(bf16)], axis=1)
    back = lax.all_to_all(back, "z", 0, 0, tiled=True)
    start_low = from_chunks(back[:, :64])
    end_low = from_chunks(back[:, 64:])

    grad_b = grad_b + lax.dot_general(xs, end_low, (((1,), (1,)), ((), ())), preferred_element_type=f32)
    grad_c = grad_c + lax.dot_general(dys, start_low, (((1,), (1,)), ((), ())), preferred_element_type=f32)
    bc_grad = jnp.concatenate([grad_b, grad_c], axis=1)
    bc_low = bc_grad.astype(bf16)
    shares = lax.all_to_all(bc_low.reshape(BLOCK, Y, 64).transpose(1, 0, 2), "y", 0, 0, tiled=True)
    carried = jnp.dot(b_proj, end_low, preferred_element_type=f32) * col_weight
    input_grad = (inner + carried).astype(bf16)

    term = jnp.einsum("ytr,ygtf->rgf", shares, everything.reshape(Y, X * CORE, BLOCK, 512), preferred_element_type=f32)
    term = term.astype(bf16).reshape(Z, 4, 4096)
    parts = lax.all_to_all(term, "z", 0, 0, tiled=True)
    weight = jnp.sum(parts.astype(f32), axis=0) / (BLOCK * Y * Z)
    return input_grad, bc_grad, weight[None]


def solution(mesh):
    fine = Mesh(mesh.devices.reshape(Y, Z, X, CORE), ("y", "z", "x", "core"))
    seq, head = ("y", "z"), ("x", "core")
    tokens = P(seq, head)
    in_specs = (tokens, tokens, tokens, tokens, P(head, seq), P(head), P(head), tokens)
    out_specs = (tokens, tokens, P(head, seq, None))
    return jax.shard_map(local, mesh=fine, in_specs=in_specs, out_specs=out_specs, check_vma=False)
```

time: 1010 us -> 170 us (0.17)
  the two profiles are of different devices: /device:TPU:2 before, /device:TPU:66 now
where the time goes in v1:
time: 170 us; the launch traced here: 169 us
  waiting for transfers between devices  76 us (45%)
  starting transfers between devices  29.6 us (17%)
  blocking collectives  23.4 us (14%)
  between operations  14.6 us (9%)
  matrix products  10.1 us (6%)
  local copies, waits for them, and re-layouts  9.87 us (6%)
  other arithmetic  5.75 us (3%)
    all_to_all x1, waiting for transfers between devices, local(): got = lax.all_to_all(packed, 'z', 0, 0, tiled=True)  28.6 us
    all_to_all x1, waiting for transfers between devices, local(): back = lax.all_to_all(back, 'z', 0, 0, tiled=True)  24.4 us
    all_to_all x1, waiting for transfers between devices, local(): parts = lax.all_to_all(term, 'z', 0, 0, tiled=True)  22.4 us
    all_to_all x1, starting transfers between devices, local(): got = lax.all_to_all(packed, 'z', 0, 0, tiled=True)  14.8 us
    all_gather x1, blocking collectives, local(): rows = lax.all_gather(totals, 'y')  14 us
    all_to_all x1, blocking collectives, local(): lax.all_to_all(bc_low.reshape(BLOCK, Y, 64).transpose(1, 0, 2), 'y', 0, 0...  9.37 us
    all_to_all x1, starting transfers between devices, local(): back = lax.all_to_all(back, 'z', 0, 0, tiled=True)  8.13 us
    all_to_all x1, starting transfers between devices, local(): parts = lax.all_to_all(term, 'z', 0, 0, tiled=True)  6.68 us
  transfers between devices with their start and end apart: 4, of which 3 were waited for; matrix products, arithmetic and copies ran while one was open for 11% of the time, Pallas kernels for 0%

profile of v1, /device:TPU:66, one launch (start us, length us, event | category | flops | bytes accessed | tf_op | source)
XLA Modules:
  0.0 169.3 jit_solution(7145290435748750764)
XLA Ops:
  7.2 0.0 copy-start
  7.2 0.0 copy-start.1
  7.2 0.0 all-gather.4.cloned.1.call-start
  7.2 0.7 all-gather.4.cloned.1.call-update
  7.9 1.2 copy.35
  9.2 0.7 exponential_negate_fusion
  9.8 0.8 copy_bitcast_fusion.1
  10.6 0.6 reduce-window.6
  11.2 0.2 slice_reduce_fusion
  11.4 1.2 copy.37
  12.7 0.1 copy_bitcast_fusion
  12.7 0.2 slice_reduce_fusion.1
  12.9 0.1 broadcast_in_dim.56
  13.0 0.8 exponential_bitcast_fusion
  13.8 0.2 fusion.13
  14.0 0.0 copy-done
  14.0 0.3 fusion.10
  14.3 0.1 copy.38
  14.6 0.0 copy-done.1
  14.6 0.3 fusion.11
  14.9 0.1 copy.40
  15.2 0.1 broadcast_in_dim.57
  15.3 0.1 broadcast_in_dim.58
  15.4 2.3 %concatenate.20 = bf16[16,136,128]{2,1,0:T(8,128)(2,1)} concatenate(bf16[16,64,128]{2,1,0:T(8,128)(2,1)S(1)} %bitcast.367, bf16[16,64,128]{2,1,0:T(8,128)(2,1)S(1)} %bitcast.368, bf16[16,1,128]{2,1,0:T(2,128)(2,1)S(1)} %convert_element_type.161, bf16[16,1,128]{2,1,0:T(2,128)(2,1)S(1)} %get-tuple-element.66, bf16[16,1,128]{2,1,0:T(2,128)(2,1)S(1)} %get-tuple-element.65, ...), dimensions={1} | concatenate | bytes 1114112 | tf_op jit(solution)/shard_map/concatenate | solution.py:49
  17.7 14.8 %all-to-all-start = ((bf16[16,136,128]{2,1,0:T(8,128)(2,1)}), bf16[16,136,128]{2,1,0:T(8,128)(2,1)S(1)}, u32[]{:S(2)}, u32[]{:S(2)}) async-start(bf16[16,136,128]{2,1,0:T(8,128)(2,1)} %concatenate.20), calls=%async_computation | async-start | bytes 1114112 | tf_op jit(solution)/shard_map/all_to_all | solution.py:52
  32.4 0.1 pad.9.clone
  32.5 28.6 %all-to-all-done = bf16[16,136,128]{2,1,0:T(8,128)(2,1)S(1)} async-done(((bf16[16,136,128]{2,1,0:T(8,128)(2,1)}), bf16[16,136,128]{2,1,0:T(8,128)(2,1)S(1)}, u32[]{:S(2)}, u32[]{:S(2)}) %all-to-all-start) | async-done | bytes 557088 | tf_op jit(solution)/shard_map/all_to_all | solution.py:52
  61.3 0.1 slice_convert_fusion.1
  61.4 0.1 fusion.34
  61.4 0.1 fusion.35
  61.5 0.0 copy-start.2
  61.5 0.1 maximum_maximum_fusion
  61.6 14.0 %all-gather = f32[544,128]{1,0:T(8,128)S(1)} all-gather(f32[136,128]{1,0:T(8,128)S(1)} %maximum_maximum_fusion), channel_id=2, replica_groups=mesh['y'=4,'z'=16,'x'=4,'core'=2] {'y'}, dimensions={0}, use_global_device_ids=true | all-gather | bytes 348160 | tf_op jit(solution)/shard_map/all_gather | solution.py:81
  76.1 0.1 add_convert_fusion
  76.2 0.1 add_convert_fusion.1
  76.3 0.8 pad_maximum_fusion
  77.1 8.1 %all-to-all-start.1 = ((bf16[16,128,128]{2,1,0:T(8,128)(2,1)}), bf16[16,128,128]{2,1,0:T(8,128)(2,1)S(1)}, u32[]{:S(2)}, u32[]{:S(2)}) async-start(bf16[16,128,128]{2,1,0:T(8,128)(2,1)} %pad_maximum_fusion), calls=%async_computation.1 | async-start | bytes 1048576 | tf_op jit(solution)/shard_map/all_to_all | solution.py:95
  85.3 0.0 copy-done.2
  85.3 1.7 %multiply_reduce_fusion = bf16[256,256]{1,0:T(8,128)(2,1)S(1)} fusion(bf16[256,16,64]{0,2,1:T(8,128)(2,1)S(1)} %bitcast.361, bf16[256,16,64]{0,2,1:T(8,128)(2,1)S(1)} %bitcast.365, f32[16,256]{1,0:T(8,128)S(1)} %copy-done.2, f32[16,256]{1,0:T(8,128)S(1)} %copy_bitcast_fusion, pred[256,256]{1,0:T(8,128)(4,1)S(1)} %iota_compare_fusion), kind=kOutput, calls=%fused_computation | convolution fusion | flops 140443648 | bytes 1277952 | tf_op jit(solution)/shard_map/shp,rhp->hsr/dot_general | solution.py:63
  87.0 0.2 fusion.74
  87.2 0.2 fusion.75
  87.5 24.4 %all-to-all-done.1 = bf16[16,128,128]{2,1,0:T(8,128)(2,1)S(1)} async-done(((bf16[16,128,128]{2,1,0:T(8,128)(2,1)}), bf16[16,128,128]{2,1,0:T(8,128)(2,1)S(1)}, u32[]{:S(2)}, u32[]{:S(2)}) %all-to-all-start.1) | async-done | bytes 524320 | tf_op jit(solution)/shard_map/all_to_all | solution.py:95
  111.9 0.2 copy.42
  112.1 0.2 copy.44
  112.2 0.2 fusion.71
  112.5 0.2 fusion.72
  112.8 9.4 %all_to_all.20 = bf16[4,256,64]{1,2,0:T(8,128)(2,1)S(1)} all-to-all(bf16[4,256,64]{1,2,0:T(8,128)(2,1)S(1)} %maximum_bitcast_fusion), channel_id=1, replica_groups=mesh['y'=4,'z'=16,'x'=4,'core'=2] {'y'}, dimensions={0} | all-to-all | bytes 262144 | tf_op jit(solution)/shard_map/all_to_all | solution.py:103
  122.1 0.0 all-gather.4.cloned.1.call-done
  122.1 0.0 copy-start.3
  122.1 5.0 %fusion.8 = bf16[64,8,512]{2,0,1:T(8,128)(2,1)S(1)} fusion(bf16[4,8,256,512]{3,2,1,0:T(8,128)(2,1)} %bitcast.360, bf16[4,256,64]{1,2,0:T(8,128)(2,1)S(1)} %all_to_all.20), kind=kOutput, calls=%fused_computation.17 | convolution fusion | flops 537133056 | bytes 9043968 | tf_op jit(solution)/shard_map/ytr,ygtf->rgf/dot_general | solution.py:107
  127.1 0.3 copy.46
  127.4 1.2 reshape.1733
  128.6 6.7 %all-to-all-start.3 = ((bf16[16,4,4096]{2,1,0:T(4,128)(2,1)}), bf16[16,4,4096]{2,1,0:T(4,128)(2,1)S(1)}, u32[]{:S(2)}, u32[]{:S(2)}) async-start(bf16[16,4,4096]{2,1,0:T(4,128)(2,1)} %reshape.1733), calls=%async_computation.3 | async-start | bytes 1048576 | tf_op jit(solution)/shard_map/all_to_all | solution.py:109
  135.2 0.0 copy-done.3
  135.2 0.1 broadcast_in_dim.53
  135.3 0.1 mul.705
  135.4 0.2 fusion.73
  135.6 1.4 fusion
  137.0 0.4 fusion.9
  137.4 1.0 copy.47
  138.4 0.8 copy.48
  139.2 22.4 %all-to-all-done.3 = bf16[16,4,4096]{2,1,0:T(4,128)(2,1)S(1)} async-done(((bf16[16,4,4096]{2,1,0:T(4,128)(2,1)}), bf16[16,4,4096]{2,1,0:T(4,128)(2,1)S(1)}, u32[]{:S(2)}, u32[]{:S(2)}) %all-to-all-start.3) | async-done | bytes 524320 | tf_op jit(solution)/shard_map/all_to_all | solution.py:109
  161.6 0.2 convert_reduce_fusion
  161.8 0.6 multiply_bitcast_fusion
  (51 shorter events, 0.8 us)
Async XLA Ops:
  7.2 6.9 %copy-start = (bf16[256,128]{1,0:T(8,128)(2,1)S(1)}, bf16[256,128]{1,0:T(8,128)(2,1)}, u32[]{:S(2)}) copy-start(bf16[256,128]{1,0:T(8,128)(2,1)} %param.10) | copy-start | bytes 196612
  7.2 7.4 %copy-start.1 = (bf16[256,128]{1,0:T(8,128)(2,1)S(1)}, bf16[256,128]{1,0:T(8,128)(2,1)}, u32[]{:S(2)}) copy-start(bf16[256,128]{1,0:T(8,128)(2,1)} %param.11) | copy-start | bytes 196612
  7.2 114.9 %all-gather.4.cloned.1.call-start = ((), (), s32[]{:S(2)}) async-start(), calls=%async_computation.4 | async-start | bytes 8650752 | tf_op jit(solution)/shard_map/all_gather | solution.py:36
  17.7 43.5 %all-to-all-start = ((bf16[16,136,128]{2,1,0:T(8,128)(2,1)}), bf16[16,136,128]{2,1,0:T(8,128)(2,1)S(1)}, u32[]{:S(2)}, u32[]{:S(2)}) async-start(bf16[16,136,128]{2,1,0:T(8,128)(2,1)} %concatenate.20), calls=%async_computation | async-start | bytes 1114112 | tf_op jit(solution)/shard_map/all_to_all | solution.py:52
  61.5 23.8 %copy-start.2 = (f32[16,256]{1,0:T(8,128)S(1)}, f32[16,256]{1,0:T(8,128)}, u32[]{:S(2)}) copy-start(f32[16,256]{1,0:T(8,128)} %param.12) | copy-start | bytes 49156
  77.1 34.7 %all-to-all-start.1 = ((bf16[16,128,128]{2,1,0:T(8,128)(2,1)}), bf16[16,128,128]{2,1,0:T(8,128)(2,1)S(1)}, u32[]{:S(2)}, u32[]{:S(2)}) async-start(bf16[16,128,128]{2,1,0:T(8,128)(2,1)} %pad_maximum_fusion), calls=%async_computation.1 | async-start | bytes 1048576 | tf_op jit(solution)/shard_map/all_to_all | solution.py:95
  122.1 13.1 %copy-start.3 = (f32[16]{0:T(128)S(1)}, f32[16]{0:T(128)}, u32[]{:S(2)}) copy-start(f32[16]{0:T(128)} %param.14) | copy-start | bytes 196
  128.6 33.0 %all-to-all-start.3 = ((bf16[16,4,4096]{2,1,0:T(4,128)(2,1)}), bf16[16,4,4096]{2,1,0:T(4,128)(2,1)S(1)}, u32[]{:S(2)}, u32[]{:S(2)}) async-start(bf16[16,4,4096]{2,1,0:T(4,128)(2,1)} %reshape.1733), calls=%async_computation.3 | async-start | bytes 1048576 | tf_op jit(solution)/shard_map/all_to_all | solution.py:109
Sparse Core Ops, SparseCore 0:
  11.2 73.7 all-gather.3

commit v2 on v1

v2 whole, which is shorter than its diff:
```python
import jax
import jax.numpy as jnp
from jax import lax
from jax.experimental import pallas as pl
from jax.experimental.pallas import tpu as pltpu
from jax.sharding import Mesh, PartitionSpec as P

Y, ZH, ZM, ZL, X, CORE = 4, 4, 2, 2, 4, 2
TOKENS = 256
HEADS = 16
PAIRS = 8
STATE = 128
LANES = 128
WIDTH = 1024
NEAR = ZM * ZL
GROUPS = Y * ZH
PART = STATE // NEAR
HALF = PART // 2
bf16 = jnp.bfloat16
f32 = jnp.float32


def dot_tt(left, right):
    return lax.dot_general(left, right, (((0,), (0,)), ((), ())), preferred_element_type=f32)


def dot_nt(left, right):
    return lax.dot_general(left, right, (((1,), (1,)), ((), ())), preferred_element_type=f32)


def dot_nn(left, right):
    return lax.dot_general(left, right, (((1,), (0,)), ((), ())), preferred_element_type=f32)


def low_lanes():
    return lax.broadcasted_iota(jnp.int32, (1, LANES), 1) < 64


def spread(columns, first, k):
    return jnp.where(low_lanes(), columns[:, first + 2 * k : first + 2 * k + 1], columns[:, first + 2 * k + 1 : first + 2 * k + 2])


def log_rows(log):
    high = log.astype(bf16).astype(f32)
    mid = (log - high).astype(bf16).astype(f32)
    low = log - high - mid
    row = lax.broadcasted_iota(jnp.int32, (8, log.shape[1]), 0)
    rows = jnp.where(row == 0, high, jnp.where(row == 1, mid, jnp.where(row == 2, low, 0.0)))
    return rows.astype(bf16)


def read_log(rows):
    return jnp.sum(rows.astype(f32), axis=0, keepdims=True)


def first_kernel(x_ref, dy_ref, b_ref, c_ref, step_ref, log_ref, packed_ref, xs_ref, dys_ref, cum_ref, cols_ref):
    step = step_ref[...]
    cum = step * -jnp.exp(log_ref[...])
    lane = lax.broadcasted_iota(jnp.int32, cum.shape, 1)
    shift = 1
    while shift < TOKENS:
        cum = cum + jnp.where(lane >= shift, pltpu.roll(cum, shift, 1), 0.0)
        shift *= 2
    cum_ref[...] = cum
    coef = jnp.exp(cum[:, TOKENS - 1 :] - cum) * step
    rows = jnp.concatenate([coef, jnp.exp(cum), cum, step, jnp.zeros((64, TOKENS), f32)], axis=0)
    cols = rows.T
    cols_ref[...] = cols
    b_t = b_ref[...].astype(f32).T.astype(bf16)
    c_t = c_ref[...].astype(f32).T.astype(bf16)
    for k in range(PAIRS):
        at = slice(k * LANES, (k + 1) * LANES)
        xs = (x_ref[:, at].astype(f32) * spread(cols, 0, k)).astype(bf16)
        dys = (dy_ref[:, at].astype(f32) * spread(cols, HEADS, k)).astype(bf16)
        xs_ref[:, at] = xs
        dys_ref[:, at] = dys
        state_in = dot_nn(b_t, xs).astype(bf16)
        state_grad = dot_nn(c_t, dys).astype(bf16)
        logs = log_rows(spread(cols[TOKENS - 1 :], 2 * HEADS, k))
        for j in range(NEAR):
            packed_ref[j, 0:PART, at] = state_in[j * PART : (j + 1) * PART]
            packed_ref[j, PART : 2 * PART, at] = state_grad[j * PART : (j + 1) * PART]
            packed_ref[j, 2 * PART : 2 * PART + 8, at] = logs


def inside_kernel(x_ref, dy_ref, b_ref, c_ref, cum_ref, cols_ref, skip_ref, inner_ref, gb_ref, gc_ref, mix_ref):
    scores = dot_nt(b_ref[...], c_ref[...])
    shape = (TOKENS, TOKENS)
    causal = lax.broadcasted_iota(jnp.int32, shape, 1) >= lax.broadcasted_iota(jnp.int32, shape, 0)
    low = low_lanes()
    low_x = low.astype(f32).astype(bf16)
    high_x = 1 - low_x
    for k in range(PAIRS):
        at = slice(k * LANES, (k + 1) * LANES)
        x = x_ref[:, at]
        dy = dy_ref[:, at]
        found = []
        for half, mask in ((0, low_x), (1, high_x)):
            h = 2 * k + half
            gaps = cum_ref[h : h + 1, :] - cols_ref[:, 2 * HEADS + h : 2 * HEADS + h + 1]
            decay = jnp.exp(jnp.where(causal, gaps, -1e30)) * cols_ref[:, 3 * HEADS + h : 3 * HEADS + h + 1]
            found.append(dot_nn((scores * decay).astype(bf16), dy))
            pairs = dot_nt(x * mask, dy) * decay
            if h == 0:
                mix_ref[...] = pairs
            else:
                mix_ref[...] += pairs
        skip = jnp.where(low, skip_ref[2 * k], skip_ref[2 * k + 1])
        inner_ref[:, at] = jnp.where(low, found[0], found[1]) + skip * dy.astype(f32)
    mix = mix_ref[...].astype(bf16)
    gb_ref[...] = dot_nn(mix, c_ref[...])
    gc_ref[...] = dot_tt(mix, b_ref[...])


def near_totals_kernel(got_ref, out_ref):
    for k in range(PAIRS):
        at = slice(k * LANES, (k + 1) * LANES)
        logs = [read_log(got_ref[m, 2 * PART : 2 * PART + 8, at]) for m in range(NEAR)]
        total = got_ref[0, 0:PART, at].astype(f32)
        for m in range(1, NEAR):
            total = jnp.exp(logs[m]) * total + got_ref[m, 0:PART, at].astype(f32)
        back = got_ref[NEAR - 1, PART : 2 * PART, at].astype(f32)
        for m in reversed(range(NEAR - 1)):
            back = jnp.exp(logs[m]) * back + got_ref[m, PART : 2 * PART, at].astype(f32)
        total, back = total.astype(bf16), back.astype(bf16)
        rows = log_rows(sum(logs[1:], logs[0]))
        for n in range(2):
            out_ref[2 * k + n, 0:HALF] = total[n * HALF : (n + 1) * HALF]
            out_ref[2 * k + n, HALF : 2 * HALF] = back[n * HALF : (n + 1) * HALF]
            out_ref[2 * k + n, 2 * HALF : 2 * HALF + 8] = rows


def far_scan_kernel(got_ref, out_ref):
    decays = [jnp.exp(read_log(got_ref[r, 2 * HALF : 2 * HALF + 8])) for r in range(GROUPS)]
    carry = jnp.zeros((HALF, LANES), f32)
    for r in range(GROUPS):
        out_ref[r, 0:HALF] = carry.astype(bf16)
        carry = decays[r] * carry + got_ref[r, 0:HALF].astype(f32)
    carry = jnp.zeros((HALF, LANES), f32)
    for r in reversed(range(GROUPS)):
        out_ref[r, HALF : 2 * HALF] = carry.astype(bf16)
        carry = decays[r] * carry + got_ref[r, HALF : 2 * HALF].astype(f32)


def near_scan_kernel(carry_ref, got_ref, out_ref):
    for k in range(PAIRS):
        at = slice(k * LANES, (k + 1) * LANES)
        decays = [jnp.exp(read_log(got_ref[m, 2 * PART : 2 * PART + 8, at])) for m in range(NEAR)]
        state = jnp.concatenate([carry_ref[2 * k + n, 0:HALF].astype(f32) for n in range(2)], axis=0)
        for m in range(NEAR):
            out_ref[m, 0:PART, at] = state.astype(bf16)
            state = decays[m] * state + got_ref[m, 0:PART, at].astype(f32)
        state = jnp.concatenate([carry_ref[2 * k + n, HALF : 2 * HALF].astype(f32) for n in range(2)], axis=0)
        for m in reversed(range(NEAR)):
            out_ref[m, PART : 2 * PART, at] = state.astype(bf16)
            state = decays[m] * state + got_ref[m, PART : 2 * PART, at].astype(f32)


def bc_kernel(states_ref, xs_ref, dys_ref, gb_ref, gc_ref, bc_ref, shares_ref):
    start = states_ref[:, 0:PART, :].reshape(STATE, WIDTH)
    end = states_ref[:, PART : 2 * PART, :].reshape(STATE, WIDTH)
    for n, (base, scaled, state) in enumerate(((gb_ref, xs_ref, end), (gc_ref, dys_ref, start))):
        grad = base[...] + dot_nt(scaled[...], state)
        bc_ref[:, n * STATE : (n + 1) * STATE] = grad
        turned = grad.T.astype(bf16)
        for half in range(2):
            for z in range(ZL):
                shares_ref[(2 * n + half) * ZL + z] = turned[half * 64 : (half + 1) * 64]


def input_kernel(states_ref, b_ref, cols_ref, inner_ref, out_ref):
    cols = cols_ref[...]
    for k in range(PAIRS):
        at = slice(k * LANES, (k + 1) * LANES)
        end = states_ref[:, PART : 2 * PART, at].reshape(STATE, LANES)
        carried = dot_nn(b_ref[...], end) * spread(cols, 0, k)
        out_ref[:, at] = (inner_ref[:, at] + carried).astype(bf16)


def weight_kernel(shares_ref, layer_ref, out_ref):
    total = dot_nn(shares_ref[0], layer_ref[0, 0, 0])
    for i in range(1, Y * ZL):
        total += dot_nn(shares_ref[i], layer_ref[i // ZL, 0, i % ZL])
    out_ref[...] = total.astype(bf16)


def call(kernel, outs, flops, exps, **kwargs):
    return pl.pallas_call(
        kernel,
        out_shape=outs if len(outs) > 1 else outs[0],
        compiler_params=pltpu.CompilerParams(vmem_limit_bytes=24 * 1024 * 1024),
        cost_estimate=pl.CostEstimate(flops=flops, bytes_accessed=2 << 20, transcendentals=exps),
        **kwargs,
    )


def shape(dims, dtype):
    return jax.ShapeDtypeStruct(dims, dtype)


def local(head_input, out_grad, b_proj, c_proj, time_step, decay_log, skip_gain, layer_input):
    halves = layer_input.reshape(TOKENS, ZL, 256).transpose(1, 0, 2)
    halves = lax.all_to_all(halves, "zl", 0, 0, tiled=True)
    layer = lax.all_gather(halves, ("y", "x", "core")).reshape(Y, X * CORE, ZL, TOKENS, 256)

    packed, xs, dys, cum, cols = call(
        first_kernel,
        (
            shape((NEAR, 2 * PART + 8, WIDTH), bf16),
            shape((TOKENS, WIDTH), bf16),
            shape((TOKENS, WIDTH), bf16),
            shape((HEADS, TOKENS), f32),
            shape((TOKENS, LANES), f32),
        ),
        1 << 28,
        1 << 13,
    )(head_input, out_grad, b_proj, c_proj, time_step, decay_log.reshape(HEADS, 1))
    near = lax.all_to_all(packed, ("zm", "zl"), 0, 0, tiled=True)

    vmem = pl.BlockSpec(memory_space=pltpu.VMEM)
    inner, grad_b, grad_c = call(
        inside_kernel,
        (shape((TOKENS, WIDTH), f32), shape((TOKENS, STATE), f32), shape((TOKENS, STATE), f32)),
        1 << 30,
        1 << 20,
        in_specs=[vmem] * 6 + [pl.BlockSpec(memory_space=pltpu.SMEM)],
        scratch_shapes=[pltpu.VMEM((TOKENS, TOKENS), f32)],
    )(head_input, out_grad, b_proj, c_proj, cum, cols, skip_gain)

    totals = call(near_totals_kernel, (shape((GROUPS, 2 * HALF + 8, LANES), bf16),), 1 << 18, 1 << 12)(near)
    far = lax.all_to_all(totals, ("y", "zh"), 0, 0, tiled=True)
    carries = call(far_scan_kernel, (shape((GROUPS, 2 * HALF, LANES), bf16),), 1 << 18, 1 << 12)(far)
    carries = lax.all_to_all(carries, ("y", "zh"), 0, 0, tiled=True)
    states = call(near_scan_kernel, (shape((NEAR, 2 * PART, WIDTH), bf16),), 1 << 18, 1 << 12)(carries, near)
    states = lax.all_to_all(states, ("zm", "zl"), 0, 0, tiled=True)

    bc_grad, shares = call(
        bc_kernel, (shape((TOKENS, 2 * STATE), f32), shape((Y * ZL, 64, TOKENS), bf16)), 1 << 27, 0
    )(states, xs, dys, grad_b, grad_c)
    shares = lax.all_to_all(shares, ("y", "zl"), 0, 0, tiled=True)
    input_grad = call(input_kernel, (shape((TOKENS, WIDTH), bf16),), 1 << 27, 0)(states, b_proj, cols, inner)

    term = call(
        weight_kernel,
        (shape((64, X * CORE * 256), bf16),),
        1 << 29,
        0,
        grid=(X * CORE,),
        in_specs=[
            pl.BlockSpec((Y * ZL, 64, TOKENS), lambda g: (0, 0, 0)),
            pl.BlockSpec((Y, 1, ZL, TOKENS, 256), lambda g: (0, g, 0, 0, 0)),
        ],
        out_specs=pl.BlockSpec((64, 256), lambda g: (0, g)),
    )(shares, layer)
    parts = lax.all_to_all(term.reshape(16, 4, X * CORE * 256), ("zh", "zm", "zl"), 0, 0, tiled=True)
    parts = parts.reshape(ZH * ZM, ZL, 4, X * CORE, 256).astype(f32)
    weight = jnp.sum(parts, axis=0).transpose(1, 2, 0, 3).reshape(4, 4096) / (TOKENS * Y * ZH * ZM * ZL)
    return input_grad, bc_grad, weight[None]


def solution(mesh):
    fine = Mesh(mesh.devices.reshape(Y, ZH, ZM, ZL, X, CORE), ("y", "zh", "zm", "zl", "x", "core"))
    seq, head = ("y", "zh", "zm", "zl"), ("x", "core")
    tokens = P(seq, head)
    in_specs = (tokens, tokens, tokens, tokens, P(head, seq), P(head), P(head), tokens)
    out_specs = (tokens, tokens, P(head, seq, None))
    return jax.shard_map(local, mesh=fine, in_specs=in_specs, out_specs=out_specs, check_vma=False)
```

time: 170 us -> 164 us (0.965)
  the two profiles are of different devices: /device:TPU:66 before, /device:TPU:32 now
where the time goes in v2:
time: 164 us; the launch traced here: 163 us
  blocking collectives  91.9 us (56%)
  waiting for transfers between devices  19.7 us (12%)
  local copies, waits for them, and re-layouts  16.6 us (10%)
  between operations  14.1 us (9%)
  Pallas kernels  12.1 us (7%)
  starting transfers between devices  8.45 us (5%)
    all_to_all x1, blocking collectives, local(): far = lax.all_to_all(totals, ('y', 'zh'), 0, 0, tiled=True)  34.9 us
    all_to_all x1, blocking collectives, local(): carries = lax.all_to_all(carries, ('y', 'zh'), 0, 0, tiled=True)  19.6 us
    all_to_all x1, waiting for transfers between devices, local(): lax.all_to_all(term.reshape(16, 4, X * CORE * 256), ('zh', 'zm', 'zl'), 0...  16.3 us
    all_to_all x1, blocking collectives, local(): near = lax.all_to_all(packed, ('zm', 'zl'), 0, 0, tiled=True)  14.7 us
    unnamed x25, local copies, waits for them, and re-layouts  13.4 us
    all_to_all x1, blocking collectives, local(): shares = lax.all_to_all(shares, ('y', 'zl'), 0, 0, tiled=True)  11.7 us
    all_to_all x1, blocking collectives, local(): halves = lax.all_to_all(halves, 'zl', 0, 0, tiled=True)  11 us
    all_to_all x1, starting transfers between devices, local(): lax.all_to_all(term.reshape(16, 4, X * CORE * 256), ('zh', 'zm', 'zl'), 0...  4.49 us
  transfers between devices with their start and end apart: 3, of which 2 were waited for; matrix products, arithmetic and copies ran while one was open for 0% of the time, Pallas kernels for 6%

profile of v2, /device:TPU:32, one launch (start us, length us, event | category | flops | bytes accessed | tf_op | source)
XLA Modules:
  0.0 162.9 jit_solution(688443633753290865)
XLA Ops:
  7.2 0.0 all-gather.3.cloned.1.call-start
  7.2 1.1 copy.15
  8.3 11.0 %all_to_all.35 = bf16[2,256,256]{1,2,0:T(8,128)(2,1)S(1)} all-to-all(bf16[2,256,256]{1,2,0:T(8,128)(2,1)S(1)} %bitcast.8), channel_id=1, replica_groups=mesh['y'=4,'zh'=4,'zm'=2,'zl'=2,'x'=4,'core'=2] {'zl'}, dimensions={0} | all-to-all | bytes 524288 | tf_op jit(solution)/shard_map/all_to_all | solution.py:203
  19.3 0.8 copy.16
  20.2 0.0 all-gather.3.cloned.1.call-update
  20.2 0.7 copy.14.log_ref
  20.9 0.0 copy-start.1
  20.9 1.0 copy-done.1
  22.0 0.0 copy-start.3
  22.0 1.0 copy-done.3
  23.0 0.0 copy-start.5
  23.0 0.8 copy-done.5
  23.9 0.0 copy-start.8
  23.9 0.8 copy-done.8
  24.7 0.0 copy-start.10
  24.7 0.7 copy-done.10
  25.4 2.3 %shard_map.103 = (bf16[4,72,1024]{2,1,0:T(8,128)(2,1)S(1)}, bf16[256,1024]{1,0:T(8,128)(2,1)S(1)}, bf16[256,1024]{1,0:T(8,128)(2,1)S(1)}, f32[16,256]{1,0:T(8,128)S(1)}, f32[256,128]{1,0:T(8,128)S(1)}) custom-call(bf16[256,1024]{1,0:T(8,128)(2,1)S(1)} %copy-done.1, bf16[256,1024]{1,0:T(8,128)(2,1)S(1)} %copy-done.3, bf16[256,128]{1,0:T(8,128)(2,1)S(1)} %copy-done.5, ...), custom_call_target="tpu_custom_call" | custom-call | flops 268435456 | bytes 2097152 | tf_op jit(solution)/shard_map/pallas_call | solution.py:206
  27.8 14.7 %all_to_all.36.got_ref = bf16[4,72,1024]{2,1,0:T(8,128)(2,1)S(1)} all-to-all(bf16[4,72,1024]{2,1,0:T(8,128)(2,1)S(1)} %get-tuple-element.13), channel_id=1, replica_groups=mesh['y'=4,'zh'=4,'zm'=2,'zl'=2,'x'=4,'core'=2] {'zm','zl'}, dimensions={0} | all-to-all | bytes 1179648 | tf_op jit(solution)/shard_map/all_to_all | solution.py:218
  42.4 0.2 shard_map.104
  42.6 34.9 %all_to_all.37.got_ref = bf16[16,40,128]{2,1,0:T(8,128)(2,1)S(1)} all-to-all(bf16[16,40,128]{2,1,0:T(8,128)(2,1)S(1)} %shard_map.104), channel_id=1, replica_groups=mesh['y'=4,'zh'=4,'zm'=2,'zl'=2,'x'=4,'core'=2] {'y','zh'}, dimensions={0} | all-to-all | bytes 327680 | tf_op jit(solution)/shard_map/all_to_all | solution.py:231
  77.5 0.1 shard_map.105
  77.6 19.6 %all_to_all.38.carry_ref = bf16[16,32,128]{2,1,0:T(8,128)(2,1)S(1)} all-to-all(bf16[16,32,128]{2,1,0:T(8,128)(2,1)S(1)} %shard_map.105), channel_id=1, replica_groups=mesh['y'=4,'zh'=4,'zm'=2,'zl'=2,'x'=4,'core'=2] {'y','zh'}, dimensions={0} | all-to-all | bytes 262144 | tf_op jit(solution)/shard_map/all_to_all | solution.py:233
  97.2 1.0 shard_map.106
  98.1 0.0 copy-start.7
  98.1 3.9 %all-to-all-start.3 = ((bf16[4,64,1024]{2,1,0:T(8,128)(2,1)}), bf16[4,64,1024]{2,1,0:T(8,128)(2,1)S(1)}, u32[]{:S(2)}, u32[]{:S(2)}) async-start(bf16[4,64,1024]{2,1,0:T(8,128)(2,1)} %shard_map.106), calls=%async_computation.3 | async-start | bytes 1048576 | tf_op jit(solution)/shard_map/all_to_all | solution.py:235
  102.1 0.0 copy-start.2
  102.1 1.0 copy-done.2
  103.1 0.0 copy-start.4
  103.1 1.0 copy-done.4
  104.2 0.0 copy-start.6
  104.2 0.8 copy-done.6
  105.0 0.0 copy-start.9
  105.0 0.8 copy-done.9
  105.8 0.0 copy-start.11
  105.8 0.7 copy-done.11
  106.5 2.8 %shard_map.107 = (f32[256,1024]{1,0:T(8,128)S(1)}, f32[256,128]{1,0:T(8,128)S(1)}, f32[256,128]{1,0:T(8,128)S(1)}) custom-call(bf16[256,1024]{1,0:T(8,128)(2,1)S(1)} %copy-done.2, bf16[256,1024]{1,0:T(8,128)(2,1)S(1)} %copy-done.4, bf16[256,128]{1,0:T(8,128)(2,1)S(1)} %copy-done.6, bf16[256,128]{1,0:T(8,128)(2,1)S(1)} %copy-done.9, ...), custom_call_target="tpu_custom_call" | custom-call | flops 1073741824 | bytes 2097152 | tf_op jit(solution)/shard_map/pallas_call | solution.py:221
  109.3 3.4 %all-to-all-done.3.states_ref = bf16[4,64,1024]{2,1,0:T(8,128)(2,1)S(1)} async-done(((bf16[4,64,1024]{2,1,0:T(8,128)(2,1)}), bf16[4,64,1024]{2,1,0:T(8,128)(2,1)S(1)}, u32[]{:S(2)}, u32[]{:S(2)}) %all-to-all-start.3) | async-done | bytes 524320 | tf_op jit(solution)/shard_map/all_to_all | solution.py:235
  112.7 1.1 shard_map.109
  113.8 11.7 %all_to_all.39.shares_ref = bf16[8,64,256]{2,1,0:T(8,128)(2,1)S(1)} all-to-all(bf16[8,64,256]{2,1,0:T(8,128)(2,1)S(1)} %get-tuple-element.22), channel_id=1, replica_groups=mesh['y'=4,'zh'=4,'zm'=2,'zl'=2,'x'=4,'core'=2] {'y','zl'}, dimensions={0} | all-to-all | bytes 524288 | tf_op jit(solution)/shard_map/all_to_all | solution.py:240
  125.5 0.0 all-gather.3.cloned.1.call-done
  125.5 0.0 copy-start
  125.5 3.4 %copy-done = bf16[64,256,256]{2,1,0:T(8,128)(2,1)S(1)} copy-done((bf16[64,256,256]{2,1,0:T(8,128)(2,1)S(1)}, bf16[64,256,256]{2,1,0:T(8,128)(2,1)}, u32[]{:S(2)}) %copy-start) | copy-done | bytes 8388632
  128.9 3.1 %shard_map.110 = bf16[64,2048]{1,0:T(8,128)(2,1)S(1)} custom-call(bf16[8,64,256]{2,1,0:T(8,128)(2,1)S(1)} %all_to_all.39.shares_ref, bf16[4,8,2,256,256]{4,3,2,1,0:T(8,128)(2,1)S(1)} %bitcast.7), custom_call_target="tpu_custom_call" | custom-call | flops 536870912 | bytes 2097152 | tf_op jit(solution)/shard_map/pallas_call | solution.py:243
  132.0 0.8 reshape.37
  132.8 4.5 %all-to-all-start.6 = ((bf16[16,4,2048]{2,1,0:T(4,128)(2,1)}), bf16[16,4,2048]{2,1,0:T(4,128)(2,1)S(1)}, u32[]{:S(2)}, u32[]{:S(2)}) async-start(bf16[16,4,2048]{2,1,0:T(4,128)(2,1)} %reshape.37), calls=%async_computation.6 | async-start | bytes 524288 | tf_op jit(solution)/shard_map/all_to_all | solution.py:255
  137.3 0.0 copy-done.7
  137.3 1.5 shard_map.108
  138.8 16.3 %all-to-all-done.6 = bf16[16,4,2048]{2,1,0:T(4,128)(2,1)S(1)} async-done(((bf16[16,4,2048]{2,1,0:T(4,128)(2,1)}), bf16[16,4,2048]{2,1,0:T(4,128)(2,1)S(1)}, u32[]{:S(2)}, u32[]{:S(2)}) %all-to-all-start.6) | async-done | bytes 262176 | tf_op jit(solution)/shard_map/all_to_all | solution.py:255
  155.1 0.1 reshape.38
  155.3 0.1 copy.17
  155.4 0.7 div.13
  (2 shorter events, 0.0 us)
Async XLA Ops:
  7.2 118.4 %all-gather.3.cloned.1.call-start = ((), (), s32[]{:S(2)}) async-start(), calls=%async_computation.7 | async-start | bytes 8650752 | tf_op jit(solution)/shard_map/all_gather | solution.py:204
  20.9 1.0 copy-start.1
  22.0 1.0 copy-start.3
  23.0 0.8 copy-start.5
  23.9 0.8 copy-start.8
  24.7 0.7 copy-start.10
  98.1 39.2 %copy-start.7 = (bf16[256,128]{1,0:T(8,128)(2,1)S(1)}, bf16[256,128]{1,0:T(8,128)(2,1)}, u32[]{:S(2)}) copy-start(bf16[256,128]{1,0:T(8,128)(2,1)} %b_ref.5) | copy-start | bytes 196612
  98.1 14.5 %all-to-all-start.3 = ((bf16[4,64,1024]{2,1,0:T(8,128)(2,1)}), bf16[4,64,1024]{2,1,0:T(8,128)(2,1)S(1)}, u32[]{:S(2)}, u32[]{:S(2)}) async-start(bf16[4,64,1024]{2,1,0:T(8,128)(2,1)} %shard_map.106), calls=%async_computation.3 | async-start | bytes 1048576 | tf_op jit(solution)/shard_map/all_to_all | solution.py:235
  102.1 1.0 copy-start.2
  103.1 1.0 copy-start.4
  104.2 0.8 copy-start.6
  105.0 0.8 copy-start.9
  105.8 0.7 copy-start.11
  125.5 3.4 %copy-start = (bf16[64,256,256]{2,1,0:T(8,128)(2,1)S(1)}, bf16[64,256,256]{2,1,0:T(8,128)(2,1)}, u32[]{:S(2)}) copy-start(bf16[64,256,256]{2,1,0:T(8,128)(2,1)} %all-gather.3.cloned.1.call-done) | copy-start | bytes 25165828
  132.8 22.3 %all-to-all-start.6 = ((bf16[16,4,2048]{2,1,0:T(4,128)(2,1)}), bf16[16,4,2048]{2,1,0:T(4,128)(2,1)S(1)}, u32[]{:S(2)}, u32[]{:S(2)}) async-start(bf16[16,4,2048]{2,1,0:T(4,128)(2,1)} %reshape.37), calls=%async_computation.6 | async-start | bytes 524288 | tf_op jit(solution)/shard_map/all_to_all | solution.py:255
Sparse Core Ops, SparseCore 0:
  20.3 70.1 all-gather.2

commit v3 on v2

v3 whole, which is shorter than its diff:
```python
import jax
import jax.numpy as jnp
from jax import lax
from jax.experimental import pallas as pl
from jax.experimental.pallas import tpu as pltpu
from jax.sharding import Mesh, PartitionSpec as P

Y, ZH, ZL, X, CORE = 4, 8, 2, 4, 2
TOKENS = 256
HEADS = 16
PAIRS = 8
STATE = 128
LANES = 128
WIDTH = 1024
BIG = 60 * 1024 * 1024
SMALL = 24 * 1024 * 1024
bf16 = jnp.bfloat16
f32 = jnp.float32


def dot_tt(left, right):
    return lax.dot_general(left, right, (((0,), (0,)), ((), ())), preferred_element_type=f32)


def dot_nt(left, right):
    return lax.dot_general(left, right, (((1,), (1,)), ((), ())), preferred_element_type=f32)


def dot_nn(left, right):
    return lax.dot_general(left, right, (((1,), (0,)), ((), ())), preferred_element_type=f32)


def low_lanes():
    return lax.broadcasted_iota(jnp.int32, (1, LANES), 1) < 64


def spread(columns, first, k):
    return jnp.where(low_lanes(), columns[:, first + 2 * k : first + 2 * k + 1], columns[:, first + 2 * k + 1 : first + 2 * k + 2])


def log_rows(log):
    high = log.astype(bf16).astype(f32)
    mid = (log - high).astype(bf16).astype(f32)
    low = log - high - mid
    row = lax.broadcasted_iota(jnp.int32, (8, log.shape[1]), 0)
    rows = jnp.where(row == 0, high, jnp.where(row == 1, mid, jnp.where(row == 2, low, 0.0)))
    return rows.astype(bf16)


def read_log(rows):
    return jnp.sum(rows.astype(f32), axis=0, keepdims=True)


def start_copies(sources, targets, sems):
    copies = [pltpu.make_async_copy(source, target, sems.at[i]) for i, (source, target) in enumerate(zip(sources, targets))]
    for copy in copies:
        copy.start()
    return copies


def first_kernel(x_hbm, dy_hbm, b_hbm, c_hbm, step_hbm, log_ref, send_ref, keep_ref, xs_ref, dys_ref, cum_ref, cols_ref, x_ref, dy_ref, b_ref, c_ref, step_ref, sems):
    copies = start_copies((step_hbm, b_hbm, c_hbm, x_hbm, dy_hbm), (step_ref, b_ref, c_ref, x_ref, dy_ref), sems)
    copies[0].wait()
    odd = lax.axis_index("zl") == 1
    step = step_ref[...]
    square = (HEADS, HEADS)
    same = lax.broadcasted_iota(jnp.int32, square, 0) == lax.broadcasted_iota(jnp.int32, square, 1)
    rate = jnp.sum(jnp.where(same, jnp.broadcast_to(-jnp.exp(log_ref[...]), square), 0.0), axis=1, keepdims=True)
    cum = step * rate
    lane = lax.broadcasted_iota(jnp.int32, cum.shape, 1)
    shift = 1
    while shift < TOKENS:
        cum = cum + jnp.where(lane >= shift, pltpu.roll(cum, shift, 1), 0.0)
        shift *= 2
    cum_ref[...] = cum
    coef = jnp.exp(cum[:, TOKENS - 1 :] - cum) * step
    rows = jnp.concatenate([coef, jnp.exp(cum), cum, step, jnp.zeros((64, TOKENS), f32)], axis=0)
    cols = rows.T
    cols_ref[...] = cols
    for copy in copies[1:]:
        copy.wait()
    b_t = b_ref[...].astype(f32).T.astype(bf16)
    c_t = c_ref[...].astype(f32).T.astype(bf16)
    for k in range(PAIRS):
        at = slice(k * LANES, (k + 1) * LANES)
        xs = (x_ref[:, at].astype(f32) * spread(cols, 0, k)).astype(bf16)
        dys = (dy_ref[:, at].astype(f32) * spread(cols, HEADS, k)).astype(bf16)
        xs_ref[:, at] = xs
        dys_ref[:, at] = dys
        state_in = dot_nn(b_t, xs)
        state_grad = dot_nn(c_t, dys)
        send_ref[0:STATE, at] = jnp.where(odd, state_grad, state_in).astype(bf16)
        keep_ref[:, at] = jnp.where(odd, state_in, state_grad)
        send_ref[STATE : STATE + 8, at] = log_rows(spread(cols[TOKENS - 1 :], 2 * HEADS, k))


def inside_kernel(x_hbm, dy_hbm, b_hbm, c_hbm, cum_ref, cols_ref, skip_ref, inner_ref, gb_ref, gc_ref, mix_ref, x_ref, dy_ref, b_ref, c_ref, sems):
    copies = start_copies((b_hbm, c_hbm, x_hbm, dy_hbm), (b_ref, c_ref, x_ref, dy_ref), sems)
    for copy in copies:
        copy.wait()
    scores = dot_nt(b_ref[...], c_ref[...])
    shape = (TOKENS, TOKENS)
    causal = lax.broadcasted_iota(jnp.int32, shape, 1) >= lax.broadcasted_iota(jnp.int32, shape, 0)
    low = low_lanes()
    low_x = low.astype(f32).astype(bf16)
    high_x = 1 - low_x
    for k in range(PAIRS):
        at = slice(k * LANES, (k + 1) * LANES)
        x = x_ref[:, at]
        dy = dy_ref[:, at]
        found = []
        for half, mask in ((0, low_x), (1, high_x)):
            h = 2 * k + half
            gaps = cum_ref[h : h + 1, :] - cols_ref[:, 2 * HEADS + h : 2 * HEADS + h + 1]
            decay = jnp.exp(jnp.where(causal, gaps, -1e30)) * cols_ref[:, 3 * HEADS + h : 3 * HEADS + h + 1]
            found.append(dot_nn((scores * decay).astype(bf16), dy))
            pairs = dot_nt(x * mask, dy) * decay
            if h == 0:
                mix_ref[...] = pairs
            else:
                mix_ref[...] += pairs
        skip = jnp.where(low, skip_ref[2 * k], skip_ref[2 * k + 1])
        inner_ref[:, at] = jnp.where(low, found[0], found[1]) + skip * dy.astype(f32)
    mix = mix_ref[...].astype(bf16)
    gb_ref[...] = dot_nn(mix, c_ref[...])
    gc_ref[...] = dot_tt(mix, b_ref[...])


def pair_kernel(send_ref, keep_ref, got_ref, out_ref):
    for k in range(PAIRS):
        at = slice(k * LANES, (k + 1) * LANES)
        own = read_log(send_ref[STATE : STATE + 8, at])
        out_ref[k, 0:STATE] = (keep_ref[:, at] + jnp.exp(own) * got_ref[0:STATE, at].astype(f32)).astype(bf16)
        out_ref[k, STATE : STATE + 8] = log_rows(own + read_log(got_ref[STATE : STATE + 8, at]))


def halves_kernel(layer_ref, other_ref, out_ref):
    columns = pl.ds(pl.multiple_of(lax.axis_index("zl") * 256, 256), 256)
    out_ref[0] = layer_ref[:, columns]
    out_ref[1] = other_ref[:, columns]


def ordered(odd, i, size):
    return odd * i + (1 - odd) * (size - 1 - i)


def total_kernel(got_ref, out_ref):
    odd = lax.axis_index("zl")
    total = jnp.zeros((STATE, LANES), f32)
    for i in range(ZH):
        z = ordered(odd, i, ZH)
        total = jnp.exp(read_log(got_ref[z, STATE : STATE + 8])) * total + got_ref[z, 0:STATE].astype(f32)
    total = total.astype(bf16)
    logs = [read_log(got_ref[z, STATE : STATE + 8]) for z in range(ZH)]
    rows = log_rows(sum(logs[1:], logs[0]))
    for y in range(Y):
        out_ref[y, 0:STATE] = total
        out_ref[y, STATE : STATE + 8] = rows


def scan_kernel(rows_ref, got_ref, out_ref):
    odd = lax.axis_index("zl")
    before = ordered(odd, lax.axis_index("y"), Y)
    state = jnp.zeros((STATE, LANES), f32)
    for i in range(Y - 1):
        y = ordered(odd, i, Y)
        later = jnp.exp(read_log(rows_ref[y, STATE : STATE + 8])) * state + rows_ref[y, 0:STATE].astype(f32)
        state = jnp.where(i < before, later, state)
    for i in range(ZH):
        z = ordered(odd, i, ZH)
        out_ref[z] = state.astype(bf16)
        if i < ZH - 1:
            state = jnp.exp(read_log(got_ref[z, STATE : STATE + 8])) * state + got_ref[z, 0:STATE].astype(f32)


def bc_kernel(carry_ref, other_ref, got_ref, xs_ref, dys_ref, gb_ref, gc_ref, bc_ref, shares_ref, end_ref, start_ref):
    odd = lax.axis_index("zl") == 1
    for k in range(PAIRS):
        at = slice(k * LANES, (k + 1) * LANES)
        decay = jnp.exp(read_log(got_ref[STATE : STATE + 8, at]))
        own = got_ref[0:STATE, at].astype(f32) + decay * carry_ref[k].astype(f32)
        other = other_ref[k].astype(f32)
        start_ref[:, at] = jnp.where(odd, own, other).astype(bf16)
        end_ref[:, at] = jnp.where(odd, other, own).astype(bf16)
    for n, (base, scaled, state) in enumerate(((gb_ref, xs_ref, end_ref), (gc_ref, dys_ref, start_ref))):
        grad = base[...] + dot_nt(scaled[...], state[...])
        bc_ref[:, n * STATE : (n + 1) * STATE] = grad
        turned = grad.T.astype(bf16)
        for half in range(2):
            for z in range(ZL):
                shares_ref[(2 * n + half) * ZL + z] = turned[half * 64 : (half + 1) * 64]


def input_kernel(end_ref, b_ref, cols_ref, inner_ref, out_ref):
    cols = cols_ref[...]
    for k in range(PAIRS):
        at = slice(k * LANES, (k + 1) * LANES)
        carried = dot_nn(b_ref[...], end_ref[:, at]) * spread(cols, 0, k)
        out_ref[:, at] = (inner_ref[:, at] + carried).astype(bf16)


def fetch_kernel(in_ref, out_ref, sem):
    copy = pltpu.make_async_copy(in_ref, out_ref, sem)
    copy.start()
    copy.wait()


def weight_kernel(shares_ref, layer_ref, out_ref):
    odd = lax.axis_index("zl")
    shares = [shares_ref[y * ZL + (odd if z == 0 else 1 - odd)] for y in range(Y) for z in range(ZL)]
    for g in range(X * CORE):
        total = dot_nn(shares[0], layer_ref[0, g, 0])
        for i in range(1, Y * ZL):
            total += dot_nn(shares[i], layer_ref[i // ZL, g, i % ZL])
        out_ref[:, g * 256 : (g + 1) * 256] = total.astype(bf16)


def call(kernel, outs, flops, exps, ins, limit=SMALL, **kwargs):
    return pl.pallas_call(
        kernel,
        out_shape=outs if len(outs) > 1 else outs[0],
        in_specs=ins,
        compiler_params=pltpu.CompilerParams(vmem_limit_bytes=limit),
        cost_estimate=pl.CostEstimate(flops=flops, bytes_accessed=2 << 20, transcendentals=exps),
        **kwargs,
    )


def shape(dims, dtype):
    return jax.ShapeDtypeStruct(dims, dtype)


def local(head_input, out_grad, b_proj, c_proj, time_step, decay_log, skip_gain, layer_input):
    vmem = pl.BlockSpec(memory_space=pltpu.VMEM)
    smem = pl.BlockSpec(memory_space=pltpu.SMEM)
    anywhere = pl.BlockSpec(memory_space=pl.ANY)
    hbm = pl.BlockSpec(memory_space=pltpu.HBM)
    swap = [(0, 1), (1, 0)]
    layer_other = lax.ppermute(layer_input, "zl", swap)

    send, keep, xs, dys, cum, cols = call(
        first_kernel,
        (
            shape((STATE + 8, WIDTH), bf16),
            shape((STATE, WIDTH), f32),
            shape((TOKENS, WIDTH), bf16),
            shape((TOKENS, WIDTH), bf16),
            shape((HEADS, TOKENS), f32),
            shape((TOKENS, LANES), f32),
        ),
        1 << 28,
        1 << 13,
        [hbm] * 5 + [vmem],
        scratch_shapes=[
            pltpu.VMEM((TOKENS, WIDTH), bf16),
            pltpu.VMEM((TOKENS, WIDTH), bf16),
            pltpu.VMEM((TOKENS, STATE), bf16),
            pltpu.VMEM((TOKENS, STATE), bf16),
            pltpu.VMEM((HEADS, TOKENS), f32),
            pltpu.SemaphoreType.DMA((5,)),
        ],
        limit=BIG,
    )(head_input, out_grad, b_proj, c_proj, time_step, decay_log.reshape(1, HEADS))
    send, layer_other = lax.optimization_barrier((send, layer_other))
    got = lax.ppermute(send, "zl", swap)
    halves = call(halves_kernel, (shape((ZL, TOKENS, 256), bf16),), 1 << 10, 0, [vmem] * 2)(
        layer_input, layer_other
    )
    layer = lax.all_gather(halves, ("y", "x", "core")).reshape(Y, X * CORE, ZL, TOKENS, 256)

    pair = call(pair_kernel, (shape((PAIRS, STATE + 8, LANES), bf16),), 1 << 18, 1 << 12, [vmem] * 3, BIG)(send, keep, got)
    far = lax.all_to_all(pair, "zh", 0, 0, tiled=True)

    inner, grad_b, grad_c = call(
        inside_kernel,
        (shape((TOKENS, WIDTH), f32), shape((TOKENS, STATE), f32), shape((TOKENS, STATE), f32)),
        1 << 30,
        1 << 20,
        [hbm] * 4 + [vmem] * 2 + [smem],
        scratch_shapes=[
            pltpu.VMEM((TOKENS, TOKENS), f32),
            pltpu.VMEM((TOKENS, WIDTH), bf16),
            pltpu.VMEM((TOKENS, WIDTH), bf16),
            pltpu.VMEM((TOKENS, STATE), bf16),
            pltpu.VMEM((TOKENS, STATE), bf16),
            pltpu.SemaphoreType.DMA((4,)),
        ],
    )(head_input, out_grad, b_proj, c_proj, cum, cols, skip_gain)

    far, inner, grad_b, grad_c = lax.optimization_barrier((far, inner, grad_b, grad_c))
    rows = call(total_kernel, (shape((Y, STATE + 8, LANES), bf16),), 1 << 18, 1 << 12, [vmem])(far)
    rows = lax.all_to_all(rows, "y", 0, 0, tiled=True)
    carry = call(scan_kernel, (shape((PAIRS, STATE, LANES), bf16),), 1 << 18, 1 << 12, [vmem] * 2)(rows, far)
    carry = lax.all_to_all(carry, "zh", 0, 0, tiled=True)
    other = lax.ppermute(carry, "zl", swap)
    layer = call(
        fetch_kernel,
        (shape(layer.shape, bf16),),
        0,
        0,
        [anywhere],
        out_specs=anywhere,
        scratch_shapes=[pltpu.SemaphoreType.DMA],
    )(layer)
    other, layer = lax.optimization_barrier((other, layer))

    bc_grad, shares, end = call(
        bc_kernel,
        (
            shape((TOKENS, 2 * STATE), f32),
            shape((Y * ZL, 64, TOKENS), bf16),
            shape((STATE, WIDTH), bf16),
        ),
        1 << 27,
        0,
        [vmem] * 7,
        scratch_shapes=[pltpu.VMEM((STATE, WIDTH), bf16)],
    )(carry, other, got, xs, dys, grad_b, grad_c)
    shares = lax.all_to_all(shares, ("y", "zl"), 0, 0, tiled=True)
    input_grad = call(input_kernel, (shape((TOKENS, WIDTH), bf16),), 1 << 27, 0, [vmem] * 4)(end, b_proj, cols, inner)

    term = call(weight_kernel, (shape((64, X * CORE * 256), bf16),), 1 << 29, 0, [vmem] * 2)(shares, layer)
    parts = lax.all_to_all(term.reshape(16, 4, X * CORE * 256), ("zh", "zl"), 0, 0, tiled=True)
    parts = parts.reshape(ZH, ZL, 4, X * CORE, 256).astype(f32)
    weight = jnp.sum(parts, axis=0).transpose(1, 2, 0, 3).reshape(4, 4096) / (TOKENS * Y * ZH * ZL)
    return input_grad, bc_grad, weight[None]


def solution(mesh):
    fine = Mesh(mesh.devices.reshape(Y, ZH, ZL, X, CORE), ("y", "zh", "zl", "x", "core"))
    seq, head = ("y", "zh", "zl"), ("x", "core")
    tokens = P(seq, head)
    in_specs = (tokens, tokens, tokens, tokens, P(head, seq), P(head), P(head), tokens)
    out_specs = (tokens, tokens, P(head, seq, None))
    return jax.shard_map(local, mesh=fine, in_specs=in_specs, out_specs=out_specs, check_vma=False)
```

time: 164 us -> 151 us (0.921)
  blocking collectives: 91.9 us -> 42.6 us
  starting transfers between devices: 8.45 us -> 31.3 us
  waiting for transfers between devices: 19.7 us -> 33.4 us
  local copies, waits for them, and re-layouts: 16.6 us -> 12.8 us
  Pallas kernels: 12.1 us -> 15.7 us
    all_to_all x4 -> x2, blocking collectives: 80.2 us -> 33.4 us  [the longest x1 22.1 us: local(): carry = lax.all_to_all(carry, 'zh', 0, 0, tiled=True)]
    ppermute x0 -> x3, starting transfers between devices: none -> 13.7 us  [the longest x1 7.39 us: local(): layer_other = lax.ppermute(layer_input, 'zl', swap)]
    all_to_all x2, starting transfers between devices: 8.41 us -> 17.6 us  [the longest x1 13.1 us: local(): far = lax.all_to_all(pair, 'zh', 0, 0, tiled=True)]
    ppermute x0 -> x3, waiting for transfers between devices: none -> 8.01 us  [the longest x1 5.01 us: local(): got = lax.ppermute(send, 'zl', swap)]
    all_to_all x2, waiting for transfers between devices: 19.7 us -> 25.4 us  [the longest x1 16.1 us: local(): lax.all_to_all(term.reshape(16, 4, X * CORE * 256), ('zh', 'zl'), 0, 0, t...]
    pallas_call x6 -> x8, Pallas kernels: 8.1 us -> 11.4 us  [the longest x1 4.82 us: local(): call(first_kernel, (shape((STATE + 8, WIDTH), bf16), shape((STATE, WIDTH)...]
    all_to_all x1, blocking collectives: 11.7 us -> 9.2 us  [local(): shares = lax.all_to_all(shares, ('y', 'zl'), 0, 0, tiled=True)]
    unnamed x25 -> x30, local copies, waits for them, and re-layouts: 13.4 us -> 11.1 us
  transfers between devices with their start and end apart: 3 -> 6, of which waited for: 2 -> 4; matrix products, arithmetic and copies ran while one was open for 0% -> 0% of each run, Pallas kernels for 6% -> 8%
where the time goes in v3:
time: 151 us; the launch traced here: 150 us
  blocking collectives  42.6 us (28%)
  waiting for transfers between devices  33.4 us (22%)
  starting transfers between devices  31.3 us (21%)
  Pallas kernels  15.7 us (10%)
  between operations  14.2 us (9%)
  local copies, waits for them, and re-layouts  12.8 us (8%)
    all_to_all x1, blocking collectives, local(): carry = lax.all_to_all(carry, 'zh', 0, 0, tiled=True)  22.1 us
    all_to_all x1, waiting for transfers between devices, local(): lax.all_to_all(term.reshape(16, 4, X * CORE * 256), ('zh', 'zl'), 0, 0, t...  16.1 us
    all_to_all x1, starting transfers between devices, local(): far = lax.all_to_all(pair, 'zh', 0, 0, tiled=True)  13.1 us
    all_to_all x1, blocking collectives, local(): rows = lax.all_to_all(rows, 'y', 0, 0, tiled=True)  11.4 us
    unnamed x30, local copies, waits for them, and re-layouts  11.1 us
    all_to_all x1, waiting for transfers between devices, local(): far = lax.all_to_all(pair, 'zh', 0, 0, tiled=True)  9.32 us
    all_to_all x1, blocking collectives, local(): shares = lax.all_to_all(shares, ('y', 'zl'), 0, 0, tiled=True)  9.2 us
    ppermute x1, starting transfers between devices, local(): layer_other = lax.ppermute(layer_input, 'zl', swap)  7.39 us
  transfers between devices with their start and end apart: 6, of which 4 were waited for; matrix products, arithmetic and copies ran while one was open for 0% of the time, Pallas kernels for 8%

profile of v3, /device:TPU:32, one launch (start us, length us, event | category | flops | bytes accessed | tf_op | source)
XLA Modules:
  0.0 150.1 jit_solution(7942267597780607)
XLA Ops:
  7.2 0.0 all-gather.3.cloned.1.call-start
  7.2 7.4 %collective-permute-start = (bf16[256,512]{1,0:T(8,128)(2,1)}, bf16[256,512]{1,0:T(8,128)(2,1)S(1)}, u32[]{:S(2)}, u32[]{:S(2)}) collective-permute-start(bf16[256,512]{1,0:T(8,128)(2,1)} %layer_ref.1), channel_id=1, source_target_pairs={{0,8},{8,0},{1,9},{9,1},{2,10},{10,2},{3,11},{11,3},{4,12},{12,4},... | collective-permute-start | bytes 786440 | tf_op jit(solution)/shard_map/ppermute | solution.py:239
  14.6 4.8 %shard_map.103 = (bf16[136,1024]{1,0:T(8,128)(2,1)}, f32[128,1024]{1,0:T(8,128)}, bf16[256,1024]{1,0:T(8,128)(2,1)}, bf16[256,1024]{1,0:T(8,128)(2,1)}, f32[16,256]{1,0:T(8,128)}, /*index=5*/f32[256,128]{1,0:T(8,128)}) custom-call(bf16[256,1024]{1,0:T(8,128)(2,1)} %x_hbm.3, bf16[256,1024]{1,0:T(8,128)(2,1)} %dy_hbm.3, bf16[256,128]{1,0:T(8,128)(2,1)} %b_ref.1, ...), custom_call_target="tpu_custom_call" | custom-call | flops 268435456 | bytes 2097152 | tf_op jit(solution)/shard_map/pallas_call | solution.py:241
  19.4 0.0 collective-permute-done.other_ref
  19.4 0.0 copy-start.7
  19.5 0.9 copy-done.7
  20.4 0.7 shard_map.108
  21.1 0.0 all-gather.3.cloned.1.call-update
  21.1 3.6 %collective-permute-start.1 = (bf16[136,1024]{1,0:T(8,128)(2,1)}, bf16[136,1024]{1,0:T(8,128)(2,1)S(1)}, u32[]{:S(2)}, u32[]{:S(2)}) collective-permute-start(bf16[136,1024]{1,0:T(8,128)(2,1)} %get-tuple-element.24.send_ref), channel_id=1, source_target_pairs={{0,8},{8,0},{1,9},{9,1},{2,10},{10,2},{3,11},{11,3},{4,12},{12,4},... | collective-permute-start | bytes 835592 | tf_op jit(solution)/shard_map/ppermute | solution.py:265
  24.8 5.0 %collective-permute-done.1.got_ref = bf16[136,1024]{1,0:T(8,128)(2,1)S(1)} collective-permute-done((bf16[136,1024]{1,0:T(8,128)(2,1)}, bf16[136,1024]{1,0:T(8,128)(2,1)S(1)}, u32[]{:S(2)}, u32[]{:S(2)}) %collective-permute-start.1) | collective-permute-done | bytes 278560 | tf_op jit(solution)/shard_map/ppermute | solution.py:265
  29.8 0.0 copy-start.1
  29.8 0.7 copy-done.1
  30.5 2.0 %shard_map.104 = bf16[8,136,128]{2,1,0:T(8,128)(2,1)} custom-call(bf16[136,1024]{1,0:T(8,128)(2,1)} %get-tuple-element.24.send_ref, f32[128,1024]{1,0:T(8,128)} %get-tuple-element.25.keep_ref, bf16[136,1024]{1,0:T(8,128)(2,1)} %copy-done.1), custom_call_target="tpu_custom_call" | custom-call | flops 262144 | bytes 2097152 | tf_op jit(solution)/shard_map/pallas_call | solution.py:271
  32.5 13.1 %all-to-all-start = ((bf16[8,136,128]{2,1,0:T(8,128)(2,1)}), bf16[8,136,128]{2,1,0:T(8,128)(2,1)S(1)}, u32[]{:S(2)}, u32[]{:S(2)}) async-start(bf16[8,136,128]{2,1,0:T(8,128)(2,1)} %shard_map.104), calls=%async_computation | async-start | bytes 557056 | tf_op jit(solution)/shard_map/all_to_all | solution.py:272
  45.6 0.0 copy-start.3
  45.6 1.0 copy-done.3
  46.7 0.0 copy-start.4
  46.7 1.1 copy-done.4
  47.7 0.0 copy-start.8
  47.7 0.8 copy-done.8
  48.6 0.0 copy-start.10
  48.6 0.9 copy-done.10
  49.5 0.0 copy-start.12
  49.5 0.8 copy-done.12
  50.3 0.0 copy-start.13
  50.3 0.7 copy-done.13
  51.0 0.0 copy-start.14
  51.0 0.7 copy-done.14
  51.7 3.1 %shard_map.105 = (f32[256,1024]{1,0:T(8,128)S(1)}, f32[256,128]{1,0:T(8,128)S(1)}, f32[256,128]{1,0:T(8,128)S(1)}) custom-call(bf16[256,1024]{1,0:T(8,128)(2,1)S(1)} %copy-done.3, bf16[256,1024]{1,0:T(8,128)(2,1)S(1)} %copy-done.4, bf16[256,128]{1,0:T(8,128)(2,1)S(1)} %copy-done.8, bf16[256,128]{1,0:T(8,128)(2,1)S(1)} %copy-done.12, ...), custom_call_target="tpu_custom_call" | custom-call | flops 1073741824 | bytes 2097152 | tf_op jit(solution)/shard_map/pallas_call | solution.py:274
  54.8 9.3 %all-to-all-done.got_ref = bf16[8,136,128]{2,1,0:T(8,128)(2,1)S(1)} async-done(((bf16[8,136,128]{2,1,0:T(8,128)(2,1)}), bf16[8,136,128]{2,1,0:T(8,128)(2,1)S(1)}, u32[]{:S(2)}, u32[]{:S(2)}) %all-to-all-start) | async-done | bytes 278560 | tf_op jit(solution)/shard_map/all_to_all | solution.py:272
  64.1 0.1 shard_map.106
  64.2 11.4 %all_to_all.25.rows_ref = bf16[4,136,128]{2,1,0:T(8,128)(2,1)S(1)} all-to-all(bf16[4,136,128]{2,1,0:T(8,128)(2,1)S(1)} %shard_map.106), channel_id=1, replica_groups=mesh['y'=4,'zh'=8,'zl'=2,'x'=4,'core'=2] {'y'}, dimensions={0} | all-to-all | bytes 278528 | tf_op jit(solution)/shard_map/all_to_all | solution.py:292
  75.6 0.1 shard_map.107
  75.7 22.1 %all_to_all.26.carry_ref = bf16[8,128,128]{2,1,0:T(8,128)(2,1)S(1)} all-to-all(bf16[8,128,128]{2,1,0:T(8,128)(2,1)S(1)} %shard_map.107), channel_id=1, replica_groups=mesh['y'=4,'zh'=8,'zl'=2,'x'=4,'core'=2] {'zh'}, dimensions={0} | all-to-all | bytes 524288 | tf_op jit(solution)/shard_map/all_to_all | solution.py:294
  97.8 2.6 %collective-permute-start.2 = (bf16[8,128,128]{2,1,0:T(8,128)(2,1)S(1)}, bf16[8,128,128]{2,1,0:T(8,128)(2,1)S(1)}, u32[]{:S(2)}, u32[]{:S(2)}) collective-permute-start(bf16[8,128,128]{2,1,0:T(8,128)(2,1)S(1)} %all_to_all.26.carry_ref), channel_id=1, source_target_pairs={{0,8},{8,0},{1,9},{9,1},{2,10},{10,2},{3,11},{11,3},{4,12},{12,4},... | collective-permute-start | bytes 786440 | tf_op jit(solution)/shard_map/ppermute | solution.py:295
  100.4 0.0 all-gather.3.cloned.1.call-done
  100.4 0.0 copy-start
  100.5 3.4 %copy-done = bf16[64,256,256]{2,1,0:T(8,128)(2,1)S(1)} copy-done((bf16[64,256,256]{2,1,0:T(8,128)(2,1)S(1)}, bf16[64,256,256]{2,1,0:T(8,128)(2,1)}, u32[]{:S(2)}) %copy-start) | copy-done | bytes 8388632
  103.8 0.0 copy-start.2
  103.8 0.0 copy-start.5
  103.8 0.0 copy-start.6
  103.8 0.6 shard_map.109.layer_ref
  104.4 0.0 copy-start.9
  104.4 0.0 copy-start.11
  104.4 3.0 %collective-permute-done.2.other_ref = bf16[8,128,128]{2,1,0:T(8,128)(2,1)S(1)} collective-permute-done((bf16[8,128,128]{2,1,0:T(8,128)(2,1)S(1)}, bf16[8,128,128]{2,1,0:T(8,128)(2,1)S(1)}, u32[]{:S(2)}, u32[]{:S(2)}) %collective-permute-start.2) | collective-permute-done | bytes 262176 | tf_op jit(solution)/shard_map/ppermute | solution.py:295
  107.4 0.0 copy-done.2
  107.4 0.0 copy-done.5
  107.4 0.0 copy-done.6
  107.4 1.3 shard_map.110
  108.7 9.2 %all_to_all.27.shares_ref = bf16[8,64,256]{2,1,0:T(8,128)(2,1)S(1)} all-to-all(bf16[8,64,256]{2,1,0:T(8,128)(2,1)S(1)} %get-tuple-element.41), channel_id=1, replica_groups=mesh['y'=4,'zh'=8,'zl'=2,'x'=4,'core'=2] {'y','zl'}, dimensions={0} | all-to-all | bytes 524288 | tf_op jit(solution)/shard_map/all_to_all | solution.py:319
  117.9 1.6 %shard_map.112 = bf16[64,2048]{1,0:T(8,128)(2,1)S(1)} custom-call(bf16[8,64,256]{2,1,0:T(8,128)(2,1)S(1)} %all_to_all.27.shares_ref, bf16[4,8,2,256,256]{4,3,2,1,0:T(8,128)(2,1)S(1)} %shard_map.109.layer_ref), custom_call_target="tpu_custom_call" | custom-call | flops 536870912 | bytes 2097152 | tf_op jit(solution)/shard_map/pallas_call | solution.py:322
  119.5 0.8 reshape.33
  120.3 4.5 %all-to-all-start.4 = ((bf16[16,4,2048]{2,1,0:T(4,128)(2,1)}), bf16[16,4,2048]{2,1,0:T(4,128)(2,1)S(1)}, u32[]{:S(2)}, u32[]{:S(2)}) async-start(bf16[16,4,2048]{2,1,0:T(4,128)(2,1)} %reshape.33), calls=%async_computation.4 | async-start | bytes 524288 | tf_op jit(solution)/shard_map/all_to_all | solution.py:323
  124.8 0.0 copy-done.9
  124.8 0.0 copy-done.11
  124.8 1.5 shard_map.111
  126.2 16.1 %all-to-all-done.4 = bf16[16,4,2048]{2,1,0:T(4,128)(2,1)S(1)} async-done(((bf16[16,4,2048]{2,1,0:T(4,128)(2,1)}), bf16[16,4,2048]{2,1,0:T(4,128)(2,1)S(1)}, u32[]{:S(2)}, u32[]{:S(2)}) %all-to-all-start.4) | async-done | bytes 262176 | tf_op jit(solution)/shard_map/all_to_all | solution.py:323
  142.3 0.1 reshape.34
  142.5 0.1 copy.11
  142.6 0.7 div.13
  (2 shorter events, 0.0 us)
Async XLA Ops:
  7.2 93.3 %all-gather.3.cloned.1.call-start = ((), (), s32[]{:S(2)}) async-start(), calls=%async_computation.5 | async-start | bytes 8650752 | tf_op jit(solution)/shard_map/all_gather | solution.py:269
  7.2 12.2 %collective-permute-start = (bf16[256,512]{1,0:T(8,128)(2,1)}, bf16[256,512]{1,0:T(8,128)(2,1)S(1)}, u32[]{:S(2)}, u32[]{:S(2)}) collective-permute-start(bf16[256,512]{1,0:T(8,128)(2,1)} %layer_ref.1), channel_id=1, source_target_pairs={{0,8},{8,0},{1,9},{9,1},{2,10},{10,2},{3,11},{11,3},{4,12},{12,4},... | collective-permute-start | bytes 786440 | tf_op jit(solution)/shard_map/ppermute | solution.py:239
  19.4 1.0 copy-start.7
  21.1 8.7 %collective-permute-start.1 = (bf16[136,1024]{1,0:T(8,128)(2,1)}, bf16[136,1024]{1,0:T(8,128)(2,1)S(1)}, u32[]{:S(2)}, u32[]{:S(2)}) collective-permute-start(bf16[136,1024]{1,0:T(8,128)(2,1)} %get-tuple-element.24.send_ref), channel_id=1, source_target_pairs={{0,8},{8,0},{1,9},{9,1},{2,10},{10,2},{3,11},{11,3},{4,12},{12,4},... | collective-permute-start | bytes 835592 | tf_op jit(solution)/shard_map/ppermute | solution.py:265
  29.8 0.7 copy-start.1
  32.5 31.6 %all-to-all-start = ((bf16[8,136,128]{2,1,0:T(8,128)(2,1)}), bf16[8,136,128]{2,1,0:T(8,128)(2,1)S(1)}, u32[]{:S(2)}, u32[]{:S(2)}) async-start(bf16[8,136,128]{2,1,0:T(8,128)(2,1)} %shard_map.104), calls=%async_computation | async-start | bytes 557056 | tf_op jit(solution)/shard_map/all_to_all | solution.py:272
  45.6 1.0 copy-start.3
  46.7 1.1 copy-start.4
  47.7 0.8 copy-start.8
  48.6 0.9 copy-start.10
  49.5 0.8 copy-start.12
  50.3 0.7 copy-start.13
  51.0 0.7 copy-start.14
  97.8 9.7 %collective-permute-start.2 = (bf16[8,128,128]{2,1,0:T(8,128)(2,1)S(1)}, bf16[8,128,128]{2,1,0:T(8,128)(2,1)S(1)}, u32[]{:S(2)}, u32[]{:S(2)}) collective-permute-start(bf16[8,128,128]{2,1,0:T(8,128)(2,1)S(1)} %all_to_all.26.carry_ref), channel_id=1, source_target_pairs={{0,8},{8,0},{1,9},{9,1},{2,10},{10,2},{3,11},{11,3},{4,12},{12,4},... | collective-permute-start | bytes 786440 | tf_op jit(solution)/shard_map/ppermute | solution.py:295
  100.4 3.4 %copy-start = (bf16[64,256,256]{2,1,0:T(8,128)(2,1)S(1)}, bf16[64,256,256]{2,1,0:T(8,128)(2,1)}, u32[]{:S(2)}) copy-start(bf16[64,256,256]{2,1,0:T(8,128)(2,1)} %all-gather.3.cloned.1.call-done) | copy-start | bytes 25165828
  103.8 3.6 %copy-start.2 = (bf16[136,1024]{1,0:T(8,128)(2,1)S(1)}, bf16[136,1024]{1,0:T(8,128)(2,1)}, u32[]{:S(2)}) copy-start(bf16[136,1024]{1,0:T(8,128)(2,1)} %copy-done.1) | copy-start | bytes 835588
  103.8 3.6 %copy-start.5 = (bf16[256,1024]{1,0:T(8,128)(2,1)S(1)}, bf16[256,1024]{1,0:T(8,128)(2,1)}, u32[]{:S(2)}) copy-start(bf16[256,1024]{1,0:T(8,128)(2,1)} %get-tuple-element.34.xs_ref) | copy-start | bytes 1572868
  103.8 3.6 %copy-start.6 = (bf16[256,1024]{1,0:T(8,128)(2,1)S(1)}, bf16[256,1024]{1,0:T(8,128)(2,1)}, u32[]{:S(2)}) copy-start(bf16[256,1024]{1,0:T(8,128)(2,1)} %get-tuple-element.35.dys_ref) | copy-start | bytes 1572868
  104.4 20.4 %copy-start.9 = (bf16[256,128]{1,0:T(8,128)(2,1)S(1)}, bf16[256,128]{1,0:T(8,128)(2,1)}, u32[]{:S(2)}) copy-start(bf16[256,128]{1,0:T(8,128)(2,1)} %b_ref.1) | copy-start | bytes 196612
  104.4 20.4 %copy-start.11 = (f32[256,128]{1,0:T(8,128)S(1)}, f32[256,128]{1,0:T(8,128)}, u32[]{:S(2)}) copy-start(f32[256,128]{1,0:T(8,128)} %get-tuple-element.27.cols_ref) | copy-start | bytes 393220
  120.3 22.0 %all-to-all-start.4 = ((bf16[16,4,2048]{2,1,0:T(4,128)(2,1)}), bf16[16,4,2048]{2,1,0:T(4,128)(2,1)S(1)}, u32[]{:S(2)}, u32[]{:S(2)}) async-start(bf16[16,4,2048]{2,1,0:T(4,128)(2,1)} %reshape.33), calls=%async_computation.4 | async-start | bytes 524288 | tf_op jit(solution)/shard_map/all_to_all | solution.py:323
Sparse Core Ops, SparseCore 0:
  21.3 70.9 all-gather.2

commit v4 on v3

--- a/solution.py
+++ b/solution.py
@@ -58,7 +58,7 @@
     return copies
 
 
-def first_kernel(x_hbm, dy_hbm, b_hbm, c_hbm, step_hbm, log_ref, send_ref, keep_ref, xs_ref, dys_ref, cum_ref, cols_ref, x_ref, dy_ref, b_ref, c_ref, step_ref, sems):
+def first_kernel(x_hbm, dy_hbm, b_hbm, c_hbm, step_hbm, log_ref, send_ref, keep_ref, cum_ref, cols_ref, x_ref, dy_ref, b_ref, c_ref, step_ref, sems):
     copies = start_copies((step_hbm, b_hbm, c_hbm, x_hbm, dy_hbm), (step_ref, b_ref, c_ref, x_ref, dy_ref), sems)
     copies[0].wait()
     odd = lax.axis_index("zl") == 1
@@ -85,16 +85,16 @@
         at = slice(k * LANES, (k + 1) * LANES)
         xs = (x_ref[:, at].astype(f32) * spread(cols, 0, k)).astype(bf16)
         dys = (dy_ref[:, at].astype(f32) * spread(cols, HEADS, k)).astype(bf16)
-        xs_ref[:, at] = xs
-        dys_ref[:, at] = dys
         state_in = dot_nn(b_t, xs)
         state_grad = dot_nn(c_t, dys)
         send_ref[0:STATE, at] = jnp.where(odd, state_grad, state_in).astype(bf16)
-        keep_ref[:, at] = jnp.where(odd, state_in, state_grad)
-        send_ref[STATE : STATE + 8, at] = log_rows(spread(cols[TOKENS - 1 :], 2 * HEADS, k))
-
-
-def inside_kernel(x_hbm, dy_hbm, b_hbm, c_hbm, cum_ref, cols_ref, skip_ref, inner_ref, gb_ref, gc_ref, mix_ref, x_ref, dy_ref, b_ref, c_ref, sems):
+        keep_ref[0:STATE, at] = jnp.where(odd, state_in, state_grad)
+        log = spread(cols[TOKENS - 1 :], 2 * HEADS, k)
+        send_ref[STATE : STATE + 8, at] = log_rows(log)
+        keep_ref[STATE : STATE + 8, at] = jnp.broadcast_to(log, (8, LANES))
+
+
+def inside_kernel(x_hbm, dy_hbm, b_hbm, c_hbm, cum_ref, cols_ref, skip_ref, inner_ref, gb_ref, gc_ref, xs_ref, dys_ref, mix_ref, x_ref, dy_ref, b_ref, c_ref, sems):
     copies = start_copies((b_hbm, c_hbm, x_hbm, dy_hbm), (b_ref, c_ref, x_ref, dy_ref), sems)
     for copy in copies:
         copy.wait()
@@ -108,6 +108,8 @@
         at = slice(k * LANES, (k + 1) * LANES)
         x = x_ref[:, at]
         dy = dy_ref[:, at]
+        xs_ref[:, at] = (x.astype(f32) * spread(cols_ref, 0, k)).astype(bf16)
+        dys_ref[:, at] = (dy.astype(f32) * spread(cols_ref, HEADS, k)).astype(bf16)
         found = []
         for half, mask in ((0, low_x), (1, high_x)):
             h = 2 * k + half
@@ -126,18 +128,18 @@
     gc_ref[...] = dot_tt(mix, b_ref[...])
 
 
-def pair_kernel(send_ref, keep_ref, got_ref, out_ref):
-    for k in range(PAIRS):
-        at = slice(k * LANES, (k + 1) * LANES)
-        own = read_log(send_ref[STATE : STATE + 8, at])
-        out_ref[k, 0:STATE] = (keep_ref[:, at] + jnp.exp(own) * got_ref[0:STATE, at].astype(f32)).astype(bf16)
+def pair_kernel(keep_ref, got_ref, out_ref):
+    for k in range(PAIRS):
+        at = slice(k * LANES, (k + 1) * LANES)
+        own = keep_ref[STATE : STATE + 1, at]
+        out_ref[k, 0:STATE] = (keep_ref[0:STATE, at] + jnp.exp(own) * got_ref[0:STATE, at].astype(f32)).astype(bf16)
         out_ref[k, STATE : STATE + 8] = log_rows(own + read_log(got_ref[STATE : STATE + 8, at]))
 
 
 def halves_kernel(layer_ref, other_ref, out_ref):
     columns = pl.ds(pl.multiple_of(lax.axis_index("zl") * 256, 256), 256)
     out_ref[0] = layer_ref[:, columns]
-    out_ref[1] = other_ref[:, columns]
+    out_ref[1] = other_ref[...]
 
 
 def ordered(odd, i, size):
@@ -205,6 +207,19 @@
     copy.wait()
 
 
+def fetch(array):
+    anywhere = pl.BlockSpec(memory_space=pl.ANY)
+    return call(
+        fetch_kernel,
+        (shape(array.shape, array.dtype),),
+        0,
+        0,
+        [anywhere],
+        out_specs=anywhere,
+        scratch_shapes=[pltpu.SemaphoreType.DMA],
+    )(array)
+
+
 def weight_kernel(shares_ref, layer_ref, out_ref):
     odd = lax.axis_index("zl")
     shares = [shares_ref[y * ZL + (odd if z == 0 else 1 - odd)] for y in range(Y) for z in range(ZL)]
@@ -212,7 +227,19 @@
         total = dot_nn(shares[0], layer_ref[0, g, 0])
         for i in range(1, Y * ZL):
             total += dot_nn(shares[i], layer_ref[i // ZL, g, i % ZL])
-        out_ref[:, g * 256 : (g + 1) * 256] = total.astype(bf16)
+        for z in range(ZH * ZL):
+            out_ref[z, :, g * 256 : (g + 1) * 256] = total[4 * z : 4 * z + 4].astype(bf16)
+
+
+def sum_kernel(parts_ref, out_ref):
+    for g in range(X * CORE):
+        at = slice(g * 256, (g + 1) * 256)
+        for z in range(ZL):
+            total = parts_ref[z, :, at].astype(f32)
+            for i in range(1, ZH):
+                total += parts_ref[ZL * i + z, :, at].astype(f32)
+            first = (g * ZL + z) * 256
+            out_ref[:, first : first + 256] = total * (1.0 / (TOKENS * Y * ZH * ZL))
 
 
 def call(kernel, outs, flops, exps, ins, limit=SMALL, **kwargs):
@@ -233,18 +260,16 @@
 def local(head_input, out_grad, b_proj, c_proj, time_step, decay_log, skip_gain, layer_input):
     vmem = pl.BlockSpec(memory_space=pltpu.VMEM)
     smem = pl.BlockSpec(memory_space=pltpu.SMEM)
-    anywhere = pl.BlockSpec(memory_space=pl.ANY)
     hbm = pl.BlockSpec(memory_space=pltpu.HBM)
     swap = [(0, 1), (1, 0)]
-    layer_other = lax.ppermute(layer_input, "zl", swap)
-
-    send, keep, xs, dys, cum, cols = call(
+    away = lax.dynamic_slice_in_dim(layer_input, (1 - lax.axis_index("zl")) * 256, 256, 1)
+    layer_other = lax.ppermute(away, "zl", swap)
+
+    send, keep, cum, cols = call(
         first_kernel,
         (
             shape((STATE + 8, WIDTH), bf16),
-            shape((STATE, WIDTH), f32),
-            shape((TOKENS, WIDTH), bf16),
-            shape((TOKENS, WIDTH), bf16),
+            shape((STATE + 8, WIDTH), f32),
             shape((HEADS, TOKENS), f32),
             shape((TOKENS, LANES), f32),
         ),
@@ -268,12 +293,19 @@
     )
     layer = lax.all_gather(halves, ("y", "x", "core")).reshape(Y, X * CORE, ZL, TOKENS, 256)
 
-    pair = call(pair_kernel, (shape((PAIRS, STATE + 8, LANES), bf16),), 1 << 18, 1 << 12, [vmem] * 3, BIG)(send, keep, got)
+    got, keep = lax.optimization_barrier((got, fetch(keep)))
+    pair = call(pair_kernel, (shape((PAIRS, STATE + 8, LANES), bf16),), 1 << 18, 1 << 12, [vmem] * 2)(keep, got)
     far = lax.all_to_all(pair, "zh", 0, 0, tiled=True)
 
-    inner, grad_b, grad_c = call(
+    inner, grad_b, grad_c, xs, dys = call(
         inside_kernel,
-        (shape((TOKENS, WIDTH), f32), shape((TOKENS, STATE), f32), shape((TOKENS, STATE), f32)),
+        (
+            shape((TOKENS, WIDTH), f32),
+            shape((TOKENS, STATE), f32),
+            shape((TOKENS, STATE), f32),
+            shape((TOKENS, WIDTH), bf16),
+            shape((TOKENS, WIDTH), bf16),
+        ),
         1 << 30,
         1 << 20,
         [hbm] * 4 + [vmem] * 2 + [smem],
@@ -287,21 +319,13 @@
         ],
     )(head_input, out_grad, b_proj, c_proj, cum, cols, skip_gain)
 
-    far, inner, grad_b, grad_c = lax.optimization_barrier((far, inner, grad_b, grad_c))
+    far, inner, grad_b, grad_c, xs, dys = lax.optimization_barrier((far, inner, grad_b, grad_c, xs, dys))
     rows = call(total_kernel, (shape((Y, STATE + 8, LANES), bf16),), 1 << 18, 1 << 12, [vmem])(far)
     rows = lax.all_to_all(rows, "y", 0, 0, tiled=True)
     carry = call(scan_kernel, (shape((PAIRS, STATE, LANES), bf16),), 1 << 18, 1 << 12, [vmem] * 2)(rows, far)
     carry = lax.all_to_all(carry, "zh", 0, 0, tiled=True)
     other = lax.ppermute(carry, "zl", swap)
-    layer = call(
-        fetch_kernel,
-        (shape(layer.shape, bf16),),
-        0,
-        0,
-        [anywhere],
-        out_specs=anywhere,
-        scratch_shapes=[pltpu.SemaphoreType.DMA],
-    )(layer)
+    layer = fetch(layer)
     other, layer = lax.optimization_barrier((other, layer))
 
     bc_grad, shares, end = call(
@@ -319,10 +343,9 @@
     shares = lax.all_to_all(shares, ("y", "zl"), 0, 0, tiled=True)
     input_grad = call(input_kernel, (shape((TOKENS, WIDTH), bf16),), 1 << 27, 0, [vmem] * 4)(end, b_proj, cols, inner)
 
-    term = call(weight_kernel, (shape((64, X * CORE * 256), bf16),), 1 << 29, 0, [vmem] * 2)(shares, layer)
-    parts = lax.all_to_all(term.reshape(16, 4, X * CORE * 256), ("zh", "zl"), 0, 0, tiled=True)
-    parts = parts.reshape(ZH, ZL, 4, X * CORE, 256).astype(f32)
-    weight = jnp.sum(parts, axis=0).transpose(1, 2, 0, 3).reshape(4, 4096) / (TOKENS * Y * ZH * ZL)
+    term = call(weight_kernel, (shape((ZH * ZL, 4, X * CORE * 256), bf16),), 1 << 29, 0, [vmem] * 2)(shares, layer)
+    parts = lax.all_to_all(term, ("zh", "zl"), 0, 0, tiled=True)
+    weight = call(sum_kernel, (shape((4, X * CORE * ZL * 256), f32),), 1 << 18, 0, [vmem])(parts)
     return input_grad, bc_grad, weight[None]
 
 

time: 151 us -> 149 us (0.987)
  waiting for transfers between devices: 33.4 us -> 31.7 us
    all_to_all x1, blocking collectives: 22.1 us -> 18.8 us  [local(): carry = lax.all_to_all(carry, 'zh', 0, 0, tiled=True)]
    ppermute x1, starting transfers between devices: 2.65 us -> 5.78 us  [local(): other = lax.ppermute(carry, 'zl', swap)]
    ppermute x1, waiting for transfers between devices: 2.99 us -> 0.59 us  [local(): other = lax.ppermute(carry, 'zl', swap)]
    all_to_all x1, starting transfers between devices: 13.1 us -> 11.3 us  [local(): far = lax.all_to_all(pair, 'zh', 0, 0, tiled=True)]
    all_to_all x1, blocking collectives: 9.2 us -> 10.8 us  [local(): shares = lax.all_to_all(shares, ('y', 'zl'), 0, 0, tiled=True)]
    pallas_call x3 -> x5, Pallas kernels: 6.94 us -> 8.21 us  [the longest x1 4.63 us: local(): call(first_kernel, (shape((STATE + 8, WIDTH), bf16), shape((STATE + 8, WI...]
    unnamed x30 -> x28, local copies, waits for them, and re-layouts: 11.1 us -> 12.3 us
where the time goes in v4:
time: 149 us; the launch traced here: 148 us
  blocking collectives  41.2 us (28%)
  waiting for transfers between devices  31.7 us (21%)
  starting transfers between devices  31.2 us (21%)
  Pallas kernels  16.3 us (11%)
  between operations  14.2 us (10%)
  local copies, waits for them, and re-layouts  13.2 us (9%)
    all_to_all x1, blocking collectives, local(): carry = lax.all_to_all(carry, 'zh', 0, 0, tiled=True)  18.8 us
    all_to_all x1, waiting for transfers between devices, local(): parts = lax.all_to_all(term, ('zh', 'zl'), 0, 0, tiled=True)  16 us
    unnamed x28, local copies, waits for them, and re-layouts  12.3 us
    all_to_all x1, blocking collectives, local(): rows = lax.all_to_all(rows, 'y', 0, 0, tiled=True)  11.6 us
    all_to_all x1, starting transfers between devices, local(): far = lax.all_to_all(pair, 'zh', 0, 0, tiled=True)  11.3 us
    all_to_all x1, blocking collectives, local(): shares = lax.all_to_all(shares, ('y', 'zl'), 0, 0, tiled=True)  10.8 us
    all_to_all x1, waiting for transfers between devices, local(): far = lax.all_to_all(pair, 'zh', 0, 0, tiled=True)  9.72 us
    ppermute x1, starting transfers between devices, local(): layer_other = lax.ppermute(away, 'zl', swap)  7.39 us
  transfers between devices with their start and end apart: 6, of which 4 were waited for; matrix products, arithmetic and copies ran while one was open for 0% of the time, Pallas kernels for 8%

profile of v4, /device:TPU:32, one launch (start us, length us, event | category | flops | bytes accessed | tf_op | source)
XLA Modules:
  0.0 147.8 jit_solution(2941237679695101107)
XLA Ops:
  7.2 0.0 all-gather.3.cloned.1.call-start
  7.2 0.9 constant_dynamic-slice_fusion
  8.1 7.4 %collective-permute-start = (bf16[256,256]{1,0:T(8,128)(2,1)S(1)}, bf16[256,256]{1,0:T(8,128)(2,1)S(1)}, u32[]{:S(2)}, u32[]{:S(2)}) collective-permute-start(bf16[256,256]{1,0:T(8,128)(2,1)S(1)} %constant_dynamic-slice_fusion), channel_id=1, source_target_pairs={{0,8},{8,0},{1,9},{9,1},{2,10},{10,2},{3,11},{11,3},{4,12},{12,4},... | collective-permute-start | bytes 393224 | tf_op jit(solution)/shard_map/ppermute | solution.py:266
  15.5 4.6 %shard_map.103 = (bf16[136,1024]{1,0:T(8,128)(2,1)}, f32[136,1024]{1,0:T(8,128)}, f32[16,256]{1,0:T(8,128)}, f32[256,128]{1,0:T(8,128)}) custom-call(bf16[256,1024]{1,0:T(8,128)(2,1)} %x_hbm.3, bf16[256,1024]{1,0:T(8,128)(2,1)} %dy_hbm.3, bf16[256,128]{1,0:T(8,128)(2,1)} %b_ref.1, bf16[256,128]{1,0:T(8,128)(2,1)} %c_hbm.3, f32[16,256]{1,0:T(8,128)} %step_hbm.1, ...), custom_call_target="tpu_custom_call" | custom-call | flops 268435456 | bytes 2097152 | tf_op jit(solution)/shard_map/pallas_call | solution.py:268
  20.2 0.0 collective-permute-done.other_ref
  20.2 0.0 copy-start.1
  20.2 0.9 copy-done.1
  21.1 0.7 shard_map.109
  21.9 0.0 all-gather.3.cloned.1.call-update
  21.9 2.2 %collective-permute-start.1 = (bf16[136,1024]{1,0:T(8,128)(2,1)}, bf16[136,1024]{1,0:T(8,128)(2,1)S(1)}, u32[]{:S(2)}, u32[]{:S(2)}) collective-permute-start(bf16[136,1024]{1,0:T(8,128)(2,1)} %get-tuple-element.28), channel_id=1, source_target_pairs={{0,8},{8,0},{1,9},{9,1},{2,10},{10,2},{3,11},{11,3},{4,12},{12,4},... | collective-permute-start | bytes 835592 | tf_op jit(solution)/shard_map/ppermute | solution.py:290
  24.1 0.0 copy-start.2
  24.1 1.0 copy-done.2
  25.1 0.1 shard_map.104.keep_ref
  25.2 5.3 %collective-permute-done.1.got_ref = bf16[136,1024]{1,0:T(8,128)(2,1)S(1)} collective-permute-done((bf16[136,1024]{1,0:T(8,128)(2,1)}, bf16[136,1024]{1,0:T(8,128)(2,1)S(1)}, u32[]{:S(2)}, u32[]{:S(2)}) %collective-permute-start.1) | collective-permute-done | bytes 278560 | tf_op jit(solution)/shard_map/ppermute | solution.py:290
  30.5 0.8 shard_map.105
  31.3 11.3 %all-to-all-start = ((bf16[8,136,128]{2,1,0:T(8,128)(2,1)}), bf16[8,136,128]{2,1,0:T(8,128)(2,1)S(1)}, u32[]{:S(2)}, u32[]{:S(2)}) async-start(bf16[8,136,128]{2,1,0:T(8,128)(2,1)} %shard_map.105), calls=%async_computation | async-start | bytes 557056 | tf_op jit(solution)/shard_map/all_to_all | solution.py:298
  42.6 0.0 copy-start.3
  42.6 1.0 copy-done.3
  43.7 0.0 copy-start.4
  43.7 1.0 copy-done.4
  44.7 0.0 copy-start.5
  44.7 0.8 copy-done.5
  45.6 0.0 copy-start.7
  45.6 0.9 copy-done.7
  46.5 0.0 copy-start.11
  46.5 0.8 copy-done.11
  47.3 0.0 copy-start.12
  47.3 0.7 copy-done.12
  48.0 0.0 copy-start.13
  48.0 0.7 copy-done.13
  48.7 3.7 %shard_map.106 = (f32[256,1024]{1,0:T(8,128)S(1)}, f32[256,128]{1,0:T(8,128)S(1)}, f32[256,128]{1,0:T(8,128)S(1)}, bf16[256,1024]{1,0:T(8,128)(2,1)S(1)}, bf16[256,1024]{1,0:T(8,128)(2,1)S(1)}) custom-call(bf16[256,1024]{1,0:T(8,128)(2,1)S(1)} %copy-done.3, bf16[256,1024]{1,0:T(8,128)(2,1)S(1)} %copy-done.4, bf16[256,128]{1,0:T(8,128)(2,1)S(1)} %copy-done.5, ...), custom_call_target="tpu_custom_call" | custom-call | flops 1073741824 | bytes 2097152 | tf_op jit(solution)/shard_map/pallas_call | solution.py:300
  52.4 0.0 copy-start.9
  52.4 9.7 %all-to-all-done.got_ref = bf16[8,136,128]{2,1,0:T(8,128)(2,1)S(1)} async-done(((bf16[8,136,128]{2,1,0:T(8,128)(2,1)}), bf16[8,136,128]{2,1,0:T(8,128)(2,1)S(1)}, u32[]{:S(2)}, u32[]{:S(2)}) %all-to-all-start) | async-done | bytes 278560 | tf_op jit(solution)/shard_map/all_to_all | solution.py:298
  62.1 0.1 shard_map.107
  62.2 11.6 %all_to_all.25.rows_ref = bf16[4,136,128]{2,1,0:T(8,128)(2,1)S(1)} all-to-all(bf16[4,136,128]{2,1,0:T(8,128)(2,1)S(1)} %shard_map.107), channel_id=1, replica_groups=mesh['y'=4,'zh'=8,'zl'=2,'x'=4,'core'=2] {'y'}, dimensions={0} | all-to-all | bytes 278528 | tf_op jit(solution)/shard_map/all_to_all | solution.py:324
  73.7 0.1 shard_map.108
  73.8 18.8 %all_to_all.26.carry_ref = bf16[8,128,128]{2,1,0:T(8,128)(2,1)S(1)} all-to-all(bf16[8,128,128]{2,1,0:T(8,128)(2,1)S(1)} %shard_map.108), channel_id=1, replica_groups=mesh['y'=4,'zh'=8,'zl'=2,'x'=4,'core'=2] {'zh'}, dimensions={0} | all-to-all | bytes 524288 | tf_op jit(solution)/shard_map/all_to_all | solution.py:326
  92.7 5.8 %collective-permute-start.2 = (bf16[8,128,128]{2,1,0:T(8,128)(2,1)S(1)}, bf16[8,128,128]{2,1,0:T(8,128)(2,1)S(1)}, u32[]{:S(2)}, u32[]{:S(2)}) collective-permute-start(bf16[8,128,128]{2,1,0:T(8,128)(2,1)S(1)} %all_to_all.26.carry_ref), channel_id=1, source_target_pairs={{0,8},{8,0},{1,9},{9,1},{2,10},{10,2},{3,11},{11,3},{4,12},{12,4},... | collective-permute-start | bytes 786440 | tf_op jit(solution)/shard_map/ppermute | solution.py:327
  98.5 0.0 all-gather.3.cloned.1.call-done
  98.5 0.0 copy-done.9
  98.5 0.0 copy-start
  98.5 3.4 %copy-done = bf16[64,256,256]{2,1,0:T(8,128)(2,1)S(1)} copy-done((bf16[64,256,256]{2,1,0:T(8,128)(2,1)S(1)}, bf16[64,256,256]{2,1,0:T(8,128)(2,1)}, u32[]{:S(2)}) %copy-start) | copy-done | bytes 8388632
  101.9 0.6 shard_map.110.layer_ref
  102.4 0.0 copy-start.6
  102.5 0.0 copy-start.8
  102.5 0.6 collective-permute-done.2.other_ref
  103.1 0.0 copy-start.10
  103.1 0.9 copy-done.10
  104.0 1.3 shard_map.111
  105.2 10.8 %all_to_all.27.shares_ref = bf16[8,64,256]{2,1,0:T(8,128)(2,1)S(1)} all-to-all(bf16[8,64,256]{2,1,0:T(8,128)(2,1)S(1)} %get-tuple-element.49), channel_id=1, replica_groups=mesh['y'=4,'zh'=8,'zl'=2,'x'=4,'core'=2] {'y','zl'}, dimensions={0} | all-to-all | bytes 524288 | tf_op jit(solution)/shard_map/all_to_all | solution.py:343
  116.0 2.3 %shard_map.113 = bf16[16,4,2048]{2,1,0:T(4,128)(2,1)} custom-call(bf16[8,64,256]{2,1,0:T(8,128)(2,1)S(1)} %all_to_all.27.shares_ref, bf16[4,8,2,256,256]{4,3,2,1,0:T(8,128)(2,1)S(1)} %shard_map.110.layer_ref), custom_call_target="tpu_custom_call" | custom-call | flops 536870912 | bytes 2097152 | tf_op jit(solution)/shard_map/pallas_call | solution.py:346
  118.3 4.5 %all-to-all-start.4 = ((bf16[16,4,2048]{2,1,0:T(4,128)(2,1)}), bf16[16,4,2048]{2,1,0:T(4,128)(2,1)S(1)}, u32[]{:S(2)}, u32[]{:S(2)}) async-start(bf16[16,4,2048]{2,1,0:T(4,128)(2,1)} %shard_map.113), calls=%async_computation.4 | async-start | bytes 524288 | tf_op jit(solution)/shard_map/all_to_all | solution.py:347
  122.8 0.0 copy-done.6
  122.8 0.0 copy-done.8
  122.8 1.5 shard_map.112
  124.3 16.0 %all-to-all-done.4.parts_ref = bf16[16,4,2048]{2,1,0:T(4,128)(2,1)S(1)} async-done(((bf16[16,4,2048]{2,1,0:T(4,128)(2,1)}), bf16[16,4,2048]{2,1,0:T(4,128)(2,1)S(1)}, u32[]{:S(2)}, u32[]{:S(2)}) %all-to-all-start.4) | async-done | bytes 262176 | tf_op jit(solution)/shard_map/all_to_all | solution.py:347
  140.3 0.7 shard_map.114
Async XLA Ops:
  7.2 91.3 %all-gather.3.cloned.1.call-start = ((), (), s32[]{:S(2)}) async-start(), calls=%async_computation.5 | async-start | bytes 8650752 | tf_op jit(solution)/shard_map/all_gather | solution.py:294
  8.1 12.0 %collective-permute-start = (bf16[256,256]{1,0:T(8,128)(2,1)S(1)}, bf16[256,256]{1,0:T(8,128)(2,1)S(1)}, u32[]{:S(2)}, u32[]{:S(2)}) collective-permute-start(bf16[256,256]{1,0:T(8,128)(2,1)S(1)} %constant_dynamic-slice_fusion), channel_id=1, source_target_pairs={{0,8},{8,0},{1,9},{9,1},{2,10},{10,2},{3,11},{11,3},{4,12},{12,4},... | collective-permute-start | bytes 393224 | tf_op jit(solution)/shard_map/ppermute | solution.py:266
  20.2 1.0 copy-start.1
  21.9 8.7 %collective-permute-start.1 = (bf16[136,1024]{1,0:T(8,128)(2,1)}, bf16[136,1024]{1,0:T(8,128)(2,1)S(1)}, u32[]{:S(2)}, u32[]{:S(2)}) collective-permute-start(bf16[136,1024]{1,0:T(8,128)(2,1)} %get-tuple-element.28), channel_id=1, source_target_pairs={{0,8},{8,0},{1,9},{9,1},{2,10},{10,2},{3,11},{11,3},{4,12},{12,4},... | collective-permute-start | bytes 835592 | tf_op jit(solution)/shard_map/ppermute | solution.py:290
  24.1 1.1 copy-start.2
  31.3 30.7 %all-to-all-start = ((bf16[8,136,128]{2,1,0:T(8,128)(2,1)}), bf16[8,136,128]{2,1,0:T(8,128)(2,1)S(1)}, u32[]{:S(2)}, u32[]{:S(2)}) async-start(bf16[8,136,128]{2,1,0:T(8,128)(2,1)} %shard_map.105), calls=%async_computation | async-start | bytes 557056 | tf_op jit(solution)/shard_map/all_to_all | solution.py:298
  42.6 1.0 copy-start.3
  43.7 1.0 copy-start.4
  44.7 0.8 copy-start.5
  45.6 0.9 copy-start.7
  46.5 0.8 copy-start.11
  47.3 0.7 copy-start.12
  48.0 0.7 copy-start.13
  52.4 46.1 %copy-start.9 = (f32[256,128]{1,0:T(8,128)}, f32[256,128]{1,0:T(8,128)S(1)}, u32[]{:S(2)}) copy-start(f32[256,128]{1,0:T(8,128)S(1)} %get-tuple-element.45.gc_ref) | copy-start | bytes 393220
  92.7 10.4 %collective-permute-start.2 = (bf16[8,128,128]{2,1,0:T(8,128)(2,1)S(1)}, bf16[8,128,128]{2,1,0:T(8,128)(2,1)S(1)}, u32[]{:S(2)}, u32[]{:S(2)}) collective-permute-start(bf16[8,128,128]{2,1,0:T(8,128)(2,1)S(1)} %all_to_all.26.carry_ref), channel_id=1, source_target_pairs={{0,8},{8,0},{1,9},{9,1},{2,10},{10,2},{3,11},{11,3},{4,12},{12,4},... | collective-permute-start | bytes 786440 | tf_op jit(solution)/shard_map/ppermute | solution.py:327
  98.5 3.4 %copy-start = (bf16[64,256,256]{2,1,0:T(8,128)(2,1)S(1)}, bf16[64,256,256]{2,1,0:T(8,128)(2,1)}, u32[]{:S(2)}) copy-start(bf16[64,256,256]{2,1,0:T(8,128)(2,1)} %all-gather.3.cloned.1.call-done) | copy-start | bytes 25165828
  102.4 20.3 %copy-start.6 = (bf16[256,128]{1,0:T(8,128)(2,1)S(1)}, bf16[256,128]{1,0:T(8,128)(2,1)}, u32[]{:S(2)}) copy-start(bf16[256,128]{1,0:T(8,128)(2,1)} %b_ref.1) | copy-start | bytes 196612
  102.5 20.3 %copy-start.8 = (f32[256,128]{1,0:T(8,128)S(1)}, f32[256,128]{1,0:T(8,128)}, u32[]{:S(2)}) copy-start(f32[256,128]{1,0:T(8,128)} %get-tuple-element.33.cols_ref) | copy-start | bytes 393220
  103.1 0.9 copy-start.10
  118.3 22.0 %all-to-all-start.4 = ((bf16[16,4,2048]{2,1,0:T(4,128)(2,1)}), bf16[16,4,2048]{2,1,0:T(4,128)(2,1)S(1)}, u32[]{:S(2)}, u32[]{:S(2)}) async-start(bf16[16,4,2048]{2,1,0:T(4,128)(2,1)} %shard_map.113), calls=%async_computation.4 | async-start | bytes 524288 | tf_op jit(solution)/shard_map/all_to_all | solution.py:347
Sparse Core Ops, SparseCore 0:
  22.0 68.5 all-gather.2

commit v5 on v4

--- a/solution.py
+++ b/solution.py
@@ -175,22 +175,43 @@
             state = jnp.exp(read_log(got_ref[z, STATE : STATE + 8])) * state + got_ref[z, 0:STATE].astype(f32)
 
 
-def bc_kernel(carry_ref, other_ref, got_ref, xs_ref, dys_ref, gb_ref, gc_ref, bc_ref, shares_ref, end_ref, start_ref):
+def own_kernel(carry_ref, got_ref, xs_ref, dys_ref, gb_ref, gc_ref, own_ref, grad_ref):
     odd = lax.axis_index("zl") == 1
     for k in range(PAIRS):
         at = slice(k * LANES, (k + 1) * LANES)
         decay = jnp.exp(read_log(got_ref[STATE : STATE + 8, at]))
-        own = got_ref[0:STATE, at].astype(f32) + decay * carry_ref[k].astype(f32)
-        other = other_ref[k].astype(f32)
-        start_ref[:, at] = jnp.where(odd, own, other).astype(bf16)
-        end_ref[:, at] = jnp.where(odd, other, own).astype(bf16)
-    for n, (base, scaled, state) in enumerate(((gb_ref, xs_ref, end_ref), (gc_ref, dys_ref, start_ref))):
-        grad = base[...] + dot_nt(scaled[...], state[...])
-        bc_ref[:, n * STATE : (n + 1) * STATE] = grad
-        turned = grad.T.astype(bf16)
-        for half in range(2):
-            for z in range(ZL):
-                shares_ref[(2 * n + half) * ZL + z] = turned[half * 64 : (half + 1) * 64]
+        own_ref[:, at] = (got_ref[0:STATE, at].astype(f32) + decay * carry_ref[k].astype(f32)).astype(bf16)
+
+    @pl.when(odd)
+    def _():
+        grad_ref[...] = gc_ref[...] + dot_nt(dys_ref[...], own_ref[...])
+
+    @pl.when(jnp.logical_not(odd))
+    def _():
+        grad_ref[...] = gb_ref[...] + dot_nt(xs_ref[...], own_ref[...])
+
+
+def bc_kernel(other_ref, own_ref, grad_ref, xs_ref, dys_ref, gb_ref, gc_ref, bc_ref, shares_ref, end_ref, state_ref):
+    odd = lax.axis_index("zl") == 1
+    for k in range(PAIRS):
+        state_ref[:, k * LANES : (k + 1) * LANES] = other_ref[k]
+
+    def finish(grad_b, grad_c, end):
+        end_ref[...] = end[...]
+        for n, grad in enumerate((grad_b, grad_c)):
+            bc_ref[:, n * STATE : (n + 1) * STATE] = grad
+            turned = grad.T.astype(bf16)
+            for half in range(2):
+                for z in range(ZL):
+                    shares_ref[(2 * n + half) * ZL + z] = turned[half * 64 : (half + 1) * 64]
+
+    @pl.when(odd)
+    def _():
+        finish(gb_ref[...] + dot_nt(xs_ref[...], state_ref[...]), grad_ref[...], state_ref)
+
+    @pl.when(jnp.logical_not(odd))
+    def _():
+        finish(grad_ref[...], gc_ref[...] + dot_nt(dys_ref[...], state_ref[...]), own_ref)
 
 
 def input_kernel(end_ref, b_ref, cols_ref, inner_ref, out_ref):
@@ -326,7 +347,10 @@
     carry = lax.all_to_all(carry, "zh", 0, 0, tiled=True)
     other = lax.ppermute(carry, "zl", swap)
     layer = fetch(layer)
-    other, layer = lax.optimization_barrier((other, layer))
+    own, grad = call(
+        own_kernel, (shape((STATE, WIDTH), bf16), shape((TOKENS, STATE), f32)), 1 << 26, 0, [vmem] * 6
+    )(carry, got, xs, dys, grad_b, grad_c)
+    other, layer, own, grad = lax.optimization_barrier((other, layer, own, grad))
 
     bc_grad, shares, end = call(
         bc_kernel,
@@ -339,7 +363,7 @@
         0,
         [vmem] * 7,
         scratch_shapes=[pltpu.VMEM((STATE, WIDTH), bf16)],
-    )(carry, other, got, xs, dys, grad_b, grad_c)
+    )(other, own, grad, xs, dys, grad_b, grad_c)
     shares = lax.all_to_all(shares, ("y", "zl"), 0, 0, tiled=True)
     input_grad = call(input_kernel, (shape((TOKENS, WIDTH), bf16),), 1 << 27, 0, [vmem] * 4)(end, b_proj, cols, inner)
 

time: 149 us -> 149 us (level)
    unnamed x28 -> x32, local copies, waits for them, and re-layouts: 12.3 us -> 13.1 us
  transfers between devices with their start and end apart: 6 -> 6, of which waited for: 4 -> 3; matrix products, arithmetic and copies ran while one was open for 0% -> 0% of each run, Pallas kernels for 8% -> 8%
where the time goes in v5:
time: 149 us; the launch traced here: 148 us
  blocking collectives  40.4 us (27%)
  starting transfers between devices  31.5 us (21%)
  waiting for transfers between devices  31.2 us (21%)
  Pallas kernels  16.6 us (11%)
  between operations  14.2 us (10%)
  local copies, waits for them, and re-layouts  14 us (9%)
    all_to_all x1, blocking collectives, local(): carry = lax.all_to_all(carry, 'zh', 0, 0, tiled=True)  18.8 us
    all_to_all x1, waiting for transfers between devices, local(): parts = lax.all_to_all(term, ('zh', 'zl'), 0, 0, tiled=True)  16.1 us
    unnamed x32, local copies, waits for them, and re-layouts  13.1 us
    all_to_all x1, blocking collectives, local(): rows = lax.all_to_all(rows, 'y', 0, 0, tiled=True)  11.6 us
    all_to_all x1, starting transfers between devices, local(): far = lax.all_to_all(pair, 'zh', 0, 0, tiled=True)  11.3 us
    all_to_all x1, blocking collectives, local(): shares = lax.all_to_all(shares, ('y', 'zl'), 0, 0, tiled=True)  10 us
    all_to_all x1, waiting for transfers between devices, local(): far = lax.all_to_all(pair, 'zh', 0, 0, tiled=True)  9.73 us
    ppermute x1, starting transfers between devices, local(): layer_other = lax.ppermute(away, 'zl', swap)  7.39 us
  transfers between devices with their start and end apart: 6, of which 3 were waited for; matrix products, arithmetic and copies ran while one was open for 0% of the time, Pallas kernels for 8%

profile of v5, /device:TPU:32, one launch (start us, length us, event | category | flops | bytes accessed | tf_op | source)
XLA Modules:
  0.0 147.9 jit_solution(2699892114742759755)
XLA Ops:
  7.2 0.0 all-gather.3.cloned.1.call-start
  7.2 0.9 constant_dynamic-slice_fusion
  8.1 7.4 %collective-permute-start = (bf16[256,256]{1,0:T(8,128)(2,1)S(1)}, bf16[256,256]{1,0:T(8,128)(2,1)S(1)}, u32[]{:S(2)}, u32[]{:S(2)}) collective-permute-start(bf16[256,256]{1,0:T(8,128)(2,1)S(1)} %constant_dynamic-slice_fusion), channel_id=1, source_target_pairs={{0,8},{8,0},{1,9},{9,1},{2,10},{10,2},{3,11},{11,3},{4,12},{12,4},... | collective-permute-start | bytes 393224 | tf_op jit(solution)/shard_map/ppermute | solution.py:287
  15.5 4.6 %shard_map.103 = (bf16[136,1024]{1,0:T(8,128)(2,1)}, f32[136,1024]{1,0:T(8,128)}, f32[16,256]{1,0:T(8,128)}, f32[256,128]{1,0:T(8,128)}) custom-call(bf16[256,1024]{1,0:T(8,128)(2,1)} %x_hbm.3, bf16[256,1024]{1,0:T(8,128)(2,1)} %dy_hbm.3, bf16[256,128]{1,0:T(8,128)(2,1)} %b_ref.1, bf16[256,128]{1,0:T(8,128)(2,1)} %c_hbm.3, f32[16,256]{1,0:T(8,128)} %step_hbm.1, ...), custom_call_target="tpu_custom_call" | custom-call | flops 268435456 | bytes 2097152 | tf_op jit(solution)/shard_map/pallas_call | solution.py:289
  20.2 0.0 collective-permute-done.other_ref
  20.2 0.0 copy-start.1
  20.2 0.9 copy-done.1
  21.1 0.7 shard_map.109
  21.9 0.0 all-gather.3.cloned.1.call-update
  21.9 2.2 %collective-permute-start.1 = (bf16[136,1024]{1,0:T(8,128)(2,1)}, bf16[136,1024]{1,0:T(8,128)(2,1)S(1)}, u32[]{:S(2)}, u32[]{:S(2)}) collective-permute-start(bf16[136,1024]{1,0:T(8,128)(2,1)} %get-tuple-element.32), channel_id=1, source_target_pairs={{0,8},{8,0},{1,9},{9,1},{2,10},{10,2},{3,11},{11,3},{4,12},{12,4},... | collective-permute-start | bytes 835592 | tf_op jit(solution)/shard_map/ppermute | solution.py:311
  24.1 0.0 copy-start.2
  24.1 1.0 copy-done.2
  25.1 0.1 shard_map.104.keep_ref
  25.2 5.3 %collective-permute-done.1.got_ref = bf16[136,1024]{1,0:T(8,128)(2,1)S(1)} collective-permute-done((bf16[136,1024]{1,0:T(8,128)(2,1)}, bf16[136,1024]{1,0:T(8,128)(2,1)S(1)}, u32[]{:S(2)}, u32[]{:S(2)}) %collective-permute-start.1) | collective-permute-done | bytes 278560 | tf_op jit(solution)/shard_map/ppermute | solution.py:311
  30.5 0.8 shard_map.105
  31.3 11.3 %all-to-all-start = ((bf16[8,136,128]{2,1,0:T(8,128)(2,1)}), bf16[8,136,128]{2,1,0:T(8,128)(2,1)S(1)}, u32[]{:S(2)}, u32[]{:S(2)}) async-start(bf16[8,136,128]{2,1,0:T(8,128)(2,1)} %shard_map.105), calls=%async_computation | async-start | bytes 557056 | tf_op jit(solution)/shard_map/all_to_all | solution.py:319
  42.6 0.0 copy-start.3
  42.6 1.0 copy-done.3
  43.7 0.0 copy-start.4
  43.7 1.0 copy-done.4
  44.7 0.0 copy-start.5
  44.7 0.8 copy-done.5
  45.6 0.0 copy-start.9
  45.6 0.9 copy-done.9
  46.5 0.0 copy-start.13
  46.5 0.8 copy-done.13
  47.3 0.0 copy-start.14
  47.3 0.7 copy-done.14
  48.0 0.0 copy-start.15
  48.0 0.7 copy-done.15
  48.7 3.7 %shard_map.106 = (f32[256,1024]{1,0:T(8,128)S(1)}, f32[256,128]{1,0:T(8,128)S(1)}, f32[256,128]{1,0:T(8,128)S(1)}, bf16[256,1024]{1,0:T(8,128)(2,1)S(1)}, bf16[256,1024]{1,0:T(8,128)(2,1)S(1)}) custom-call(bf16[256,1024]{1,0:T(8,128)(2,1)S(1)} %copy-done.3, bf16[256,1024]{1,0:T(8,128)(2,1)S(1)} %copy-done.4, bf16[256,128]{1,0:T(8,128)(2,1)S(1)} %copy-done.5, ...), custom_call_target="tpu_custom_call" | custom-call | flops 1073741824 | bytes 2097152 | tf_op jit(solution)/shard_map/pallas_call | solution.py:321
  52.4 9.7 %all-to-all-done.got_ref = bf16[8,136,128]{2,1,0:T(8,128)(2,1)S(1)} async-done(((bf16[8,136,128]{2,1,0:T(8,128)(2,1)}), bf16[8,136,128]{2,1,0:T(8,128)(2,1)S(1)}, u32[]{:S(2)}, u32[]{:S(2)}) %all-to-all-start) | async-done | bytes 278560 | tf_op jit(solution)/shard_map/all_to_all | solution.py:319
  62.1 0.1 shard_map.107
  62.2 11.6 %all_to_all.25.rows_ref = bf16[4,136,128]{2,1,0:T(8,128)(2,1)S(1)} all-to-all(bf16[4,136,128]{2,1,0:T(8,128)(2,1)S(1)} %shard_map.107), channel_id=1, replica_groups=mesh['y'=4,'zh'=8,'zl'=2,'x'=4,'core'=2] {'y'}, dimensions={0} | all-to-all | bytes 278528 | tf_op jit(solution)/shard_map/all_to_all | solution.py:345
  73.7 0.1 shard_map.108
  73.8 18.8 %all_to_all.26.carry_ref = bf16[8,128,128]{2,1,0:T(8,128)(2,1)S(1)} all-to-all(bf16[8,128,128]{2,1,0:T(8,128)(2,1)S(1)} %shard_map.108), channel_id=1, replica_groups=mesh['y'=4,'zh'=8,'zl'=2,'x'=4,'core'=2] {'zh'}, dimensions={0} | all-to-all | bytes 524288 | tf_op jit(solution)/shard_map/all_to_all | solution.py:347
  92.7 5.8 %collective-permute-start.2 = (bf16[8,128,128]{2,1,0:T(8,128)(2,1)S(1)}, bf16[8,128,128]{2,1,0:T(8,128)(2,1)S(1)}, u32[]{:S(2)}, u32[]{:S(2)}) collective-permute-start(bf16[8,128,128]{2,1,0:T(8,128)(2,1)S(1)} %all_to_all.26.carry_ref), channel_id=1, source_target_pairs={{0,8},{8,0},{1,9},{9,1},{2,10},{10,2},{3,11},{11,3},{4,12},{12,4},... | collective-permute-start | bytes 786440 | tf_op jit(solution)/shard_map/ppermute | solution.py:348
  98.5 0.4 shard_map.111
  98.9 0.0 copy-start.11
  98.9 0.6 copy-done.11
  99.6 0.0 all-gather.3.cloned.1.call-done
  99.6 0.0 copy-start
  99.6 3.4 %copy-done = bf16[64,256,256]{2,1,0:T(8,128)(2,1)S(1)} copy-done((bf16[64,256,256]{2,1,0:T(8,128)(2,1)S(1)}, bf16[64,256,256]{2,1,0:T(8,128)(2,1)}, u32[]{:S(2)}) %copy-start) | copy-done | bytes 8388632
  102.9 0.0 copy-start.12
  102.9 0.6 shard_map.110.layer_ref
  103.5 0.0 copy-start.6
  103.5 0.0 copy-start.10
  103.5 0.0 collective-permute-done.2.other_ref
  103.5 0.3 copy-done.12
  103.8 1.1 shard_map.112
  105.0 0.0 copy-start.7
  105.0 0.7 copy-done.7
  105.7 0.0 copy-start.8
  105.7 10.0 %all_to_all.27.shares_ref = bf16[8,64,256]{2,1,0:T(8,128)(2,1)S(1)} all-to-all(bf16[8,64,256]{2,1,0:T(8,128)(2,1)S(1)} %get-tuple-element.57), channel_id=1, replica_groups=mesh['y'=4,'zh'=8,'zl'=2,'x'=4,'core'=2] {'y','zl'}, dimensions={0} | all-to-all | bytes 524288 | tf_op jit(solution)/shard_map/all_to_all | solution.py:367
  115.7 2.3 %shard_map.114 = bf16[16,4,2048]{2,1,0:T(4,128)(2,1)} custom-call(bf16[8,64,256]{2,1,0:T(8,128)(2,1)S(1)} %all_to_all.27.shares_ref, bf16[4,8,2,256,256]{4,3,2,1,0:T(8,128)(2,1)S(1)} %shard_map.110.layer_ref), custom_call_target="tpu_custom_call" | custom-call | flops 536870912 | bytes 2097152 | tf_op jit(solution)/shard_map/pallas_call | solution.py:370
  118.0 4.8 %all-to-all-start.4 = ((bf16[16,4,2048]{2,1,0:T(4,128)(2,1)}), bf16[16,4,2048]{2,1,0:T(4,128)(2,1)S(1)}, u32[]{:S(2)}, u32[]{:S(2)}) async-start(bf16[16,4,2048]{2,1,0:T(4,128)(2,1)} %shard_map.114), calls=%async_computation.4 | async-start | bytes 524288 | tf_op jit(solution)/shard_map/all_to_all | solution.py:371
  122.8 0.0 copy-done.6
  122.8 0.0 copy-done.10
  122.8 0.0 copy-done.8
  122.8 1.5 shard_map.113
  124.3 16.1 %all-to-all-done.4.parts_ref = bf16[16,4,2048]{2,1,0:T(4,128)(2,1)S(1)} async-done(((bf16[16,4,2048]{2,1,0:T(4,128)(2,1)}), bf16[16,4,2048]{2,1,0:T(4,128)(2,1)S(1)}, u32[]{:S(2)}, u32[]{:S(2)}) %all-to-all-start.4) | async-done | bytes 262176 | tf_op jit(solution)/shard_map/all_to_all | solution.py:371
  140.4 0.7 shard_map.115
Async XLA Ops:
  7.2 92.4 %all-gather.3.cloned.1.call-start = ((), (), s32[]{:S(2)}) async-start(), calls=%async_computation.5 | async-start | bytes 8650752 | tf_op jit(solution)/shard_map/all_gather | solution.py:315
  8.1 12.0 %collective-permute-start = (bf16[256,256]{1,0:T(8,128)(2,1)S(1)}, bf16[256,256]{1,0:T(8,128)(2,1)S(1)}, u32[]{:S(2)}, u32[]{:S(2)}) collective-permute-start(bf16[256,256]{1,0:T(8,128)(2,1)S(1)} %constant_dynamic-slice_fusion), channel_id=1, source_target_pairs={{0,8},{8,0},{1,9},{9,1},{2,10},{10,2},{3,11},{11,3},{4,12},{12,4},... | collective-permute-start | bytes 393224 | tf_op jit(solution)/shard_map/ppermute | solution.py:287
  20.2 1.0 copy-start.1
  21.9 8.7 %collective-permute-start.1 = (bf16[136,1024]{1,0:T(8,128)(2,1)}, bf16[136,1024]{1,0:T(8,128)(2,1)S(1)}, u32[]{:S(2)}, u32[]{:S(2)}) collective-permute-start(bf16[136,1024]{1,0:T(8,128)(2,1)} %get-tuple-element.32), channel_id=1, source_target_pairs={{0,8},{8,0},{1,9},{9,1},{2,10},{10,2},{3,11},{11,3},{4,12},{12,4},... | collective-permute-start | bytes 835592 | tf_op jit(solution)/shard_map/ppermute | solution.py:311
  24.1 1.1 copy-start.2
  31.3 30.7 %all-to-all-start = ((bf16[8,136,128]{2,1,0:T(8,128)(2,1)}), bf16[8,136,128]{2,1,0:T(8,128)(2,1)S(1)}, u32[]{:S(2)}, u32[]{:S(2)}) async-start(bf16[8,136,128]{2,1,0:T(8,128)(2,1)} %shard_map.105), calls=%async_computation | async-start | bytes 557056 | tf_op jit(solution)/shard_map/all_to_all | solution.py:319
  42.6 1.0 copy-start.3
  43.7 1.0 copy-start.4
  44.7 0.8 copy-start.5
  45.6 0.9 copy-start.9
  46.5 0.8 copy-start.13
  47.3 0.7 copy-start.14
  48.0 0.7 copy-start.15
  92.7 10.9 %collective-permute-start.2 = (bf16[8,128,128]{2,1,0:T(8,128)(2,1)S(1)}, bf16[8,128,128]{2,1,0:T(8,128)(2,1)S(1)}, u32[]{:S(2)}, u32[]{:S(2)}) collective-permute-start(bf16[8,128,128]{2,1,0:T(8,128)(2,1)S(1)} %all_to_all.26.carry_ref), channel_id=1, source_target_pairs={{0,8},{8,0},{1,9},{9,1},{2,10},{10,2},{3,11},{11,3},{4,12},{12,4},... | collective-permute-start | bytes 786440 | tf_op jit(solution)/shard_map/ppermute | solution.py:348
  98.9 0.7 copy-start.11
  99.6 3.4 %copy-start = (bf16[64,256,256]{2,1,0:T(8,128)(2,1)S(1)}, bf16[64,256,256]{2,1,0:T(8,128)(2,1)}, u32[]{:S(2)}) copy-start(bf16[64,256,256]{2,1,0:T(8,128)(2,1)} %all-gather.3.cloned.1.call-done) | copy-start | bytes 25165828
  102.9 0.9 copy-start.12
  103.5 19.3 %copy-start.6 = (bf16[256,128]{1,0:T(8,128)(2,1)S(1)}, bf16[256,128]{1,0:T(8,128)(2,1)}, u32[]{:S(2)}) copy-start(bf16[256,128]{1,0:T(8,128)(2,1)} %b_ref.1) | copy-start | bytes 196612
  103.5 19.3 %copy-start.10 = (f32[256,128]{1,0:T(8,128)S(1)}, f32[256,128]{1,0:T(8,128)}, u32[]{:S(2)}) copy-start(f32[256,128]{1,0:T(8,128)} %get-tuple-element.37.cols_ref) | copy-start | bytes 393220
  105.0 0.7 copy-start.7
  105.7 17.1 %copy-start.8 = (bf16[128,1024]{1,0:T(8,128)(2,1)S(1)}, bf16[128,1024]{1,0:T(8,128)(2,1)}, u32[]{:S(2)}) copy-start(bf16[128,1024]{1,0:T(8,128)(2,1)} %copy-done.7) | copy-start | bytes 786436
  118.0 22.4 %all-to-all-start.4 = ((bf16[16,4,2048]{2,1,0:T(4,128)(2,1)}), bf16[16,4,2048]{2,1,0:T(4,128)(2,1)S(1)}, u32[]{:S(2)}, u32[]{:S(2)}) async-start(bf16[16,4,2048]{2,1,0:T(4,128)(2,1)} %shard_map.114), calls=%async_computation.4 | async-start | bytes 524288 | tf_op jit(solution)/shard_map/all_to_all | solution.py:371
Sparse Core Ops, SparseCore 0:
  22.0 68.5 all-gather.2
